TPU v7x, 32 devices: a whole 2x2x4 slice. The times are simulated.
32 devices in a mesh: dp: 4 (over x, core), fsdp: 8 (over z, y).
Axes of the slice: x: 2, y: 2, z: 4, core: 2. Of those that a mesh axis runs over, the one named last changes fastest.
Arguments:
- images: bfloat16 [32, 197, 768], P(('dp', 'fsdp')), may hold values from -6 to 6
- image_cot: bfloat16 [32, 197, 768], P(('dp', 'fsdp')), may hold values from -6 to 6
- captions: bfloat16 [32, 512, 768], P(('dp', 'fsdp')), may hold values from -6 to 6
- caption_cot: bfloat16 [32, 512, 768], P(('dp', 'fsdp')), may hold values from -6 to 6
- lengths: int32 [32, 8], P(('dp', 'fsdp')), may hold values from 1 to 256, 448 in all within a row
- w_qkv: bfloat16 [2, 768, 2304], P(None, 'fsdp'), may hold values from -0.21875 to 0.21875
- w_out: bfloat16 [2, 768, 768], P(None, 'fsdp'), may hold values from -0.875 to 0.875
- w_up: bfloat16 [2, 768, 3072], P(None, 'fsdp'), may hold values from -0.21875 to 0.21875
- w_down: bfloat16 [2, 3072, 768], P(None, 'fsdp'), may hold values from -0.109375 to 0.109375
- gains: bfloat16 [2, 2, 768], P(None, None, 'fsdp'), may hold values from 0.5 to 1.5
- biases: bfloat16 [2, 6, 768], P(None, None, 'fsdp'), may hold values from -2.5 to 2.5
- b_up: bfloat16 [2, 3072], P(None, 'fsdp'), may hold values from -2.5 to 2.5
Outputs:
- image_out: bfloat16 [32, 197, 768], P(('dp', 'fsdp'))
- caption_out: bfloat16 [32, 512, 768], P(('dp', 'fsdp'))
- image_grad: float32 [32, 197, 768], P(('dp', 'fsdp'))
- caption_grad: float32 [32, 512, 768], P(('dp', 'fsdp'))
- grad_qkv: float32 [2, 768, 2304], P(None, 'fsdp')
- grad_out: float32 [2, 768, 768], P(None, 'fsdp')
- grad_up: float32 [2, 768, 3072], P(None, 'fsdp')
- grad_down: float32 [2, 3072, 768], P(None, 'fsdp')
- grad_gains: float32 [2, 2, 768], P(None, None, 'fsdp')
- grad_biases: float32 [2, 6, 768], P(None, None, 'fsdp')
- grad_bup: float32 [2, 3072], P(None, 'fsdp')
Inputs may be any that keep to these rules, and one draw needn't show every extreme that they name: The 8 lengths of each packed row sum to 448; the rest of the row is padding.
All inputs are finite; a program needn't handle non-finite values.
Results may differ from a plain program's by a relative error of at most 0.014.
Values may be sent and summed in bfloat16 or wider, within the bound.
A program may use at most 192 MiB of HBM per device.

v0:
```python
import jax
import jax.numpy as jnp
from jax import lax
from jax.sharding import PartitionSpec as P

HEAD = 64


def normed(values, gain, shift):
    center = values - jnp.mean(values, axis=-1, keepdims=True)
    spread = jnp.mean(center * center, axis=-1, keepdims=True)
    return center * lax.rsqrt(spread + 1e-05) * gain + shift


def gelu_exact(values):
    return jax.nn.gelu(values, approximate=False)


def segment_ids(lengths, seq_len):
    bounds = jnp.cumsum(lengths, axis=-1)
    positions = jnp.arange(seq_len, dtype=jnp.int32)
    return jnp.sum((positions[None, :, None] >= bounds[:, None, :]).astype(jnp.int32), axis=-1)


def split_heads(values):
    batch, length, width = values.shape
    return values.reshape(batch, length, width // HEAD, HEAD)


def masked_scores(queries, keys_all, segment):
    scores = jnp.einsum(
        "bqhd,bkhd->bhqk",
        split_heads(queries),
        split_heads(keys_all),
        preferred_element_type=jnp.float32,
    )
    same = (segment[:, :, None] == segment[:, None, :])[:, None]
    return (jnp.where(same, scores, -1e30), same)


def attention(queries, keys_all, values_all, segment):
    scores, same = masked_scores(queries, keys_all, segment)
    largest = jnp.max(scores, axis=-1, keepdims=True)
    raised = jnp.exp(scores - largest)
    totals = jnp.sum(raised, axis=-1, keepdims=True)
    attn_weights = raised / totals
    log_total = largest + jnp.log(totals)
    mixed = jnp.einsum(
        "bhqk,bkhd->bqhd",
        attn_weights.astype(jnp.bfloat16),
        split_heads(values_all),
        preferred_element_type=jnp.float32,
    )
    return (mixed.reshape(queries.shape).astype(jnp.bfloat16), log_total)


def attention_back(queries, keys_all, values_all, segment, log_total, grad_mixed):
    scores, same = masked_scores(queries, keys_all, segment)
    attn_weights = jnp.where(same, jnp.exp(scores - log_total), 0.0)
    grad_heads = split_heads(grad_mixed)
    grad_weights = jnp.einsum(
        "bqhd,bkhd->bhqk", grad_heads, split_heads(values_all), preferred_element_type=jnp.float32
    )
    inner = jnp.sum(attn_weights * grad_weights, axis=-1, keepdims=True)
    grad_scores = (attn_weights * (grad_weights - inner)).astype(jnp.bfloat16)
    grad_queries = jnp.einsum(
        "bhqk,bkhd->bqhd", grad_scores, split_heads(keys_all), preferred_element_type=jnp.float32
    )
    grad_keys = jnp.einsum(
        "bhqk,bqhd->bkhd", grad_scores, split_heads(queries), preferred_element_type=jnp.float32
    )
    grad_values = jnp.einsum(
        "bhqk,bqhd->bkhd",
        attn_weights.astype(jnp.bfloat16),
        grad_heads,
        preferred_element_type=jnp.float32,
    )
    shape_rows = queries.shape
    return (
        grad_queries.reshape(shape_rows),
        grad_keys.reshape(shape_rows),
        grad_values.reshape(shape_rows),
    )


def forward_layer(inputs, weights, segment):
    qkv_weight, out_weight, up_weight, down_weight, gains, biases, up_bias = weights
    width = inputs.shape[-1]
    source = inputs.astype(jnp.float32)
    normed_a = normed(source, gains[0], biases[0]).astype(jnp.bfloat16)
    project = jnp.einsum("bld,de->ble", normed_a, qkv_weight, preferred_element_type=jnp.float32)
    queries = ((project[..., :width] + biases[2]) * HEAD ** (-0.5)).astype(jnp.bfloat16)
    keys_all = project[..., width : 2 * width].astype(jnp.bfloat16)
    values_all = (project[..., 2 * width :] + biases[3]).astype(jnp.bfloat16)
    mixed, log_total = attention(queries, keys_all, values_all, segment)
    hidden = (
        source
        + jnp.einsum("bld,de->ble", mixed, out_weight, preferred_element_type=jnp.float32)
        + biases[4]
    )
    normed_c = normed(hidden, gains[1], biases[1]).astype(jnp.bfloat16)
    before = (
        jnp.einsum("bld,df->blf", normed_c, up_weight, preferred_element_type=jnp.float32) + up_bias
    )
    activated = gelu_exact(before).astype(jnp.bfloat16)
    result = (
        hidden
        + jnp.einsum("blf,fd->bld", activated, down_weight, preferred_element_type=jnp.float32)
        + biases[5]
    )
    return (
        source,
        normed_a,
        queries,
        keys_all,
        values_all,
        log_total,
        mixed,
        hidden,
        normed_c,
        before,
        activated,
        result,
    )


def backward_layer(inputs, cotangent, weights, segment):
    qkv_weight, out_weight, up_weight, down_weight, gains, biases, up_bias = weights
    width = inputs.shape[-1]
    (
        source,
        normed_a,
        queries,
        keys_all,
        values_all,
        log_total,
        mixed,
        hidden,
        normed_c,
        before,
        activated,
        result,
    ) = forward_layer(inputs, weights, segment)
    grad_result = cotangent.astype(jnp.float32)
    grad_downw = jnp.einsum("blf,bld->fd", activated, cotangent, preferred_element_type=jnp.float32)
    grad_act = jnp.einsum("bld,fd->blf", cotangent, down_weight, preferred_element_type=jnp.float32)
    grad_before = jax.vjp(gelu_exact, before)[1](grad_act)[0].astype(jnp.bfloat16)
    grad_upw = jnp.einsum("bld,blf->df", normed_c, grad_before, preferred_element_type=jnp.float32)
    grad_upb = jnp.sum(grad_before.astype(jnp.float32), axis=(0, 1))
    grad_normc = jnp.einsum(
        "blf,df->bld", grad_before, up_weight, preferred_element_type=jnp.float32
    )
    hidden_back = jax.vjp(
        normed, hidden, gains[1].astype(jnp.float32), biases[1].astype(jnp.float32)
    )[1]
    grad_hidden_ln, grad_gain_two, grad_shift_two = hidden_back(grad_normc)
    grad_hidden = grad_result + grad_hidden_ln
    grad_branch = grad_hidden.astype(jnp.bfloat16)
    grad_outw = jnp.einsum("bld,ble->de", mixed, grad_branch, preferred_element_type=jnp.float32)
    grad_mixed = jnp.einsum(
        "ble,de->bld", grad_branch, out_weight, preferred_element_type=jnp.float32
    ).astype(jnp.bfloat16)
    grad_queries, grad_keys, grad_values = attention_back(
        queries, keys_all, values_all, segment, log_total, grad_mixed
    )
    grad_project = jnp.concatenate(
        [
            grad_queries.astype(jnp.bfloat16) * HEAD ** (-0.5),
            grad_keys.astype(jnp.bfloat16),
            grad_values.astype(jnp.bfloat16),
        ],
        axis=-1,
    )
    grad_qkvw = jnp.einsum(
        "bld,ble->de", normed_a, grad_project, preferred_element_type=jnp.float32
    )
    column_sums = jnp.sum(grad_project.astype(jnp.float32), axis=(0, 1))
    grad_norma = jnp.einsum(
        "ble,de->bld", grad_project, qkv_weight, preferred_element_type=jnp.float32
    )
    source_back = jax.vjp(
        normed, source, gains[0].astype(jnp.float32), biases[0].astype(jnp.float32)
    )[1]
    grad_source_ln, grad_gain_one, grad_shift_one = source_back(grad_norma)
    grad_inputs = grad_hidden + grad_source_ln
    grad_gains = jnp.stack([grad_gain_one, grad_gain_two])
    grad_biases = jnp.stack(
        [
            grad_shift_one,
            grad_shift_two,
            column_sums[:width],
            column_sums[2 * width :],
            jnp.sum(grad_branch.astype(jnp.float32), axis=(0, 1)),
            jnp.sum(grad_result, axis=(0, 1)),
        ]
    )
    return (
        grad_inputs,
        (grad_qkvw, grad_outw, grad_upw, grad_downw, grad_gains, grad_biases, grad_upb),
    )


def fetch_weights(layer_index, w_qkv, w_out, w_up, w_down, gains, biases, b_up):
    return (
        lax.all_gather(w_qkv[layer_index], "fsdp", axis=0, tiled=True),
        lax.all_gather(w_out[layer_index], "fsdp", axis=0, tiled=True),
        lax.all_gather(w_up[layer_index], "fsdp", axis=0, tiled=True),
        lax.all_gather(w_down[layer_index], "fsdp", axis=0, tiled=True),
        lax.all_gather(gains[layer_index], "fsdp", axis=1, tiled=True),
        lax.all_gather(biases[layer_index], "fsdp", axis=1, tiled=True),
        lax.all_gather(b_up[layer_index], "fsdp", axis=0, tiled=True),
    )


def fetch_again(layer_index, w_qkv, w_out, w_up, w_down, gains, biases, b_up):
    return (
        lax.all_gather(w_qkv[layer_index], "fsdp", axis=0, tiled=True),
        lax.all_gather(w_out[layer_index], "fsdp", axis=0, tiled=True),
        lax.all_gather(w_up[layer_index], "fsdp", axis=0, tiled=True),
        lax.all_gather(w_down[layer_index], "fsdp", axis=0, tiled=True),
        lax.all_gather(gains[layer_index], "fsdp", axis=1, tiled=True),
        lax.all_gather(biases[layer_index], "fsdp", axis=1, tiled=True),
        lax.all_gather(b_up[layer_index], "fsdp", axis=0, tiled=True),
    )


def reduce_grads(gradients):
    shares = (
        lax.psum_scatter(gradients[0], "fsdp", scatter_dimension=0, tiled=True),
        lax.psum_scatter(gradients[1], "fsdp", scatter_dimension=0, tiled=True),
        lax.psum_scatter(gradients[2], "fsdp", scatter_dimension=0, tiled=True),
        lax.psum_scatter(gradients[3], "fsdp", scatter_dimension=0, tiled=True),
        lax.psum_scatter(gradients[4], "fsdp", scatter_dimension=1, tiled=True),
        lax.psum_scatter(gradients[5], "fsdp", scatter_dimension=1, tiled=True),
        lax.psum_scatter(gradients[6], "fsdp", scatter_dimension=0, tiled=True),
    )
    quarters = (
        lax.psum_scatter(
            shares[0].astype(jnp.bfloat16), "dp", scatter_dimension=0, tiled=True
        ).astype(jnp.float32),
        lax.psum_scatter(
            shares[1].astype(jnp.bfloat16), "dp", scatter_dimension=0, tiled=True
        ).astype(jnp.float32),
        lax.psum_scatter(
            shares[2].astype(jnp.bfloat16), "dp", scatter_dimension=0, tiled=True
        ).astype(jnp.float32),
        lax.psum_scatter(
            shares[3].astype(jnp.bfloat16), "dp", scatter_dimension=0, tiled=True
        ).astype(jnp.float32),
        lax.psum_scatter(
            shares[4].astype(jnp.bfloat16), "dp", scatter_dimension=1, tiled=True
        ).astype(jnp.float32),
        lax.psum_scatter(
            shares[5].astype(jnp.bfloat16), "dp", scatter_dimension=1, tiled=True
        ).astype(jnp.float32),
        lax.psum_scatter(
            shares[6].astype(jnp.bfloat16), "dp", scatter_dimension=0, tiled=True
        ).astype(jnp.float32),
    )
    return (
        lax.all_gather(quarters[0].astype(jnp.bfloat16), "dp", axis=0, tiled=True).astype(
            jnp.float32
        ),
        lax.all_gather(quarters[1].astype(jnp.bfloat16), "dp", axis=0, tiled=True).astype(
            jnp.float32
        ),
        lax.all_gather(quarters[2].astype(jnp.bfloat16), "dp", axis=0, tiled=True).astype(
            jnp.float32
        ),
        lax.all_gather(quarters[3].astype(jnp.bfloat16), "dp", axis=0, tiled=True).astype(
            jnp.float32
        ),
        lax.all_gather(quarters[4].astype(jnp.bfloat16), "dp", axis=1, tiled=True).astype(
            jnp.float32
        ),
        lax.all_gather(quarters[5].astype(jnp.bfloat16), "dp", axis=1, tiled=True).astype(
            jnp.float32
        ),
        lax.all_gather(quarters[6].astype(jnp.bfloat16), "dp", axis=0, tiled=True).astype(
            jnp.float32
        ),
    )


def local(
    images,
    image_cot,
    captions,
    caption_cot,
    lengths,
    w_qkv,
    w_out,
    w_up,
    w_down,
    gains,
    biases,
    b_up,
):
    owned = (w_qkv, w_out, w_up, w_down, gains, biases, b_up)
    image_seg = jnp.zeros((images.shape[0], images.shape[1]), jnp.int32)
    caption_seg = segment_ids(lengths, captions.shape[1])
    first_weights = fetch_weights(0, *owned)
    image_out = forward_layer(images, first_weights, image_seg)[-1].astype(jnp.bfloat16)
    second_weights = fetch_weights(1, *owned)
    caption_out = forward_layer(captions, second_weights, caption_seg)[-1].astype(jnp.bfloat16)
    second_back = fetch_again(1, *owned)
    caption_grad, caption_terms = backward_layer(captions, caption_cot, second_back, caption_seg)
    caption_shares = reduce_grads(caption_terms)
    first_back = fetch_again(0, *owned)
    image_grad, image_terms = backward_layer(images, image_cot, first_back, image_seg)
    image_shares = reduce_grads(image_terms)
    stacked = tuple((jnp.stack([image_shares[index], caption_shares[index]]) for index in range(7)))
    return (image_out, caption_out, image_grad, caption_grad) + stacked


def solution(mesh):
    placed = (
        P(("dp", "fsdp"), None, None),
        P(("dp", "fsdp"), None, None),
        P(("dp", "fsdp"), None, None),
        P(("dp", "fsdp"), None, None),
        P(("dp", "fsdp"), None),
        P(None, "fsdp", None),
        P(None, "fsdp", None),
        P(None, "fsdp", None),
        P(None, "fsdp", None),
        P(None, None, "fsdp"),
        P(None, None, "fsdp"),
        P(None, "fsdp"),
    )
    return jax.shard_map(
        local,
        mesh=mesh,
        in_specs=placed,
        out_specs=(
            P(("dp", "fsdp"), None, None),
            P(("dp", "fsdp"), None, None),
            P(("dp", "fsdp"), None, None),
            P(("dp", "fsdp"), None, None),
            P(None, "fsdp", None),
            P(None, "fsdp", None),
            P(None, "fsdp", None),
            P(None, "fsdp", None),
            P(None, None, "fsdp"),
            P(None, None, "fsdp"),
            P(None, "fsdp"),
        ),
        check_vma=False,
    )
```

profile of v0, /device:TPU:9, one launch (start us, length us, event | category | flops | bytes accessed | tf_op | source)
XLA Modules:
  0.0 2094.9 jit_solution(9857543846352453059)
XLA Ops:
  18.8 21.0 %all-gather.12 = bf16[1,3072]{1,0:T(2,128)(2,1)S(1)} all-gather(bf16[1,384]{1,0:T(2,128)(2,1)S(1)} %get-tuple-element.145), channel_id=14, replica_groups=mesh['dp'=4,'fsdp'=8] {'fsdp'}, dimensions={1}, use_global_device_ids=true | all-gather | bytes 6912 | tf_op jit(solution)/shard_map/all_gather | solution.py:211
  40.4 22.8 %all-gather.5 = bf16[1,3072]{1,0:T(2,128)(2,1)S(1)} all-gather(bf16[1,384]{1,0:T(2,128)(2,1)S(1)} %get-tuple-element.146), channel_id=7, replica_groups=mesh['dp'=4,'fsdp'=8] {'fsdp'}, dimensions={1}, use_global_device_ids=true | all-gather | bytes 6912 | tf_op jit(solution)/shard_map/all_gather | solution.py:211
  65.2 24.5 %all-gather = bf16[1,2,768]{1,0,2:T(2,128)(2,1)S(1)} all-gather(bf16[1,2,96]{1,0,2:T(2,128)(2,1)S(1)} %copy.192), channel_id=2, replica_groups=mesh['dp'=4,'fsdp'=8] {'fsdp'}, dimensions={2}, use_global_device_ids=true | all-gather | bytes 3456 | tf_op jit(solution)/shard_map/all_gather | solution.py:209
  94.3 26.2 %all-gather.1 = bf16[1,6,768]{1,0,2:T(2,128)(2,1)S(1)} all-gather(bf16[1,6,96]{1,0,2:T(2,128)(2,1)S(1)} %copy.193), channel_id=3, replica_groups=mesh['dp'=4,'fsdp'=8] {'fsdp'}, dimensions={2}, use_global_device_ids=true | all-gather | bytes 10368 | tf_op jit(solution)/shard_map/all_gather | solution.py:210
  120.5 14.0 fusion.135
  134.5 24.8 %all-gather.7 = bf16[1,2,768]{1,0,2:T(2,128)(2,1)S(1)} all-gather(bf16[1,2,96]{1,0,2:T(2,128)(2,1)S(1)} %copy.194), channel_id=9, replica_groups=mesh['dp'=4,'fsdp'=8] {'fsdp'}, dimensions={2}, use_global_device_ids=true | all-gather | bytes 3456 | tf_op jit(solution)/shard_map/all_gather | solution.py:209
  164.4 27.0 %all-gather.8 = bf16[1,6,768]{1,0,2:T(2,128)(2,1)S(1)} all-gather(bf16[1,6,96]{1,0,2:T(2,128)(2,1)S(1)} %copy.195), channel_id=10, replica_groups=mesh['dp'=4,'fsdp'=8] {'fsdp'}, dimensions={2}, use_global_device_ids=true | all-gather | bytes 10368 | tf_op jit(solution)/shard_map/all_gather | solution.py:210
  191.4 14.0 fusion.127
  260.7 58.2 %all-gather.31.cloned.1.call-done = bf16[1,768,3072]{2,1,0:T(8,128)(2,1)} async-done(((bf16[1,96,3072]{2,1,0:T(8,128)(2,1)}), bf16[1,768,3072]{2,1,0:T(8,128)(2,1)}) %all-gather.31.cloned.1.call-update) | async-done | bytes 4718608 | tf_op jit(solution)/shard_map/all_gather | solution.py:207
  328.6 71.0 %all-gather.33.cloned.1.call-done = bf16[1,3072,768]{2,1,0:T(8,128)(2,1)} async-done(((bf16[1,384,768]{2,1,0:T(8,128)(2,1)}), bf16[1,3072,768]{2,1,0:T(8,128)(2,1)}) %all-gather.33.cloned.1.call-update) | async-done | bytes 4718608 | tf_op jit(solution)/shard_map/all_gather | solution.py:208
  413.3 67.2 %all-gather.39.cloned.1.call-done = bf16[1,768,3072]{2,1,0:T(8,128)(2,1)} async-done(((bf16[1,96,3072]{2,1,0:T(8,128)(2,1)}), bf16[1,768,3072]{2,1,0:T(8,128)(2,1)}) %all-gather.39.cloned.1.call-update) | async-done | bytes 4718608 | tf_op jit(solution)/shard_map/all_gather | solution.py:207
  480.5 21.2 %multiply_convert_fusion.1 = (bf16[512,3072]{1,0:T(8,128)(2,1)}, f32[512,3072]{1,0:T(8,128)}, f32[512,3072]{1,0:T(8,128)}) fusion(f32[3072]{0:T(1024)} %bitcast.404, bf16[1,768,3072]{2,1,0:T(8,128)(2,1)} %all-gather.39.cloned.1.call-done, f32[1,512,768]{2,1,0:T(8,128)} %copy-done.12, f32[768]{0:T(1024)} %get-tuple-element.86, f32[768]{0:T(1024)} %get-tuple-element.91, ...), kind=kOutput, calls=%fused_computation.12 | convolution fusion | flops 2521694208 | bytes 22042624 | tf_op jit(solution)/shard_map/bld,df->blf/dot_general | solution.py:103
  501.7 59.0 %all-gather.41.cloned.1.call-done = bf16[1,3072,768]{2,1,0:T(8,128)(2,1)} async-done(((bf16[1,384,768]{2,1,0:T(8,128)(2,1)}), bf16[1,3072,768]{2,1,0:T(8,128)(2,1)}) %all-gather.41.cloned.1.call-update) | async-done | bytes 4718608 | tf_op jit(solution)/shard_map/all_gather | solution.py:208
  683.4 20.6 reduce-scatter.45.cloned.1.call-done
  705.9 130.6 %reduce-scatter.33.cloned.1.call-done = f32[96,2304]{1,0:T(8,128)} async-done(((f32[768,2304]{1,0:T(8,128)}), f32[96,2304]{1,0:T(8,128)}) %reduce-scatter.33.cloned.1.call-update) | async-done | bytes 884752 | tf_op jit(solution)/shard_map/reduce_scatter | solution.py:229
  838.6 130.0 %reduce-scatter.37.cloned.1.call-done = f32[96,2304]{1,0:T(8,128)} async-done(((f32[768,2304]{1,0:T(8,128)}), f32[96,2304]{1,0:T(8,128)}) %reduce-scatter.37.cloned.1.call-update) | async-done | bytes 884752 | tf_op jit(solution)/shard_map/reduce_scatter | solution.py:229
  979.0 155.2 %reduce-scatter.49.cloned.1.call-done = f32[96,3072]{1,0:T(8,128)} async-done(((f32[768,3072]{1,0:T(8,128)}), f32[96,3072]{1,0:T(8,128)}) %reduce-scatter.49.cloned.1.call-update) | async-done | bytes 1179664 | tf_op jit(solution)/shard_map/reduce_scatter | solution.py:231
  1141.6 29.0 %all-reduce.10 = (bf16[3072]{0:T(1024)(128)(2,1)S(1)}, bf16[3072]{0:T(1024)(128)(2,1)S(1)}) all-reduce(f32[3072]{0:T(1024)S(1)} %copy-done.98, f32[3072]{0:T(1024)S(1)} %copy-done.97), channel_id=42, replica_groups=mesh['dp'=4,'fsdp'=8] {'fsdp'}, use_global_device_ids=true, to_apply=%region_66.67.clone | all-reduce | flops 6144 | bytes 36864
  1183.5 116.8 %reduce-scatter.57.cloned.1.call-done = f32[384,768]{1,0:T(8,128)} async-done(((f32[3072,768]{1,0:T(8,128)}), f32[384,768]{1,0:T(8,128)}) %reduce-scatter.57.cloned.1.call-update) | async-done | bytes 1179664 | tf_op jit(solution)/shard_map/reduce_scatter | solution.py:232
  1312.8 50.5 %reduce-scatter.65.cloned.1.call-done = f32[96,2]{1,0:T(8,128)} async-done(((f32[768,2]{1,0:T(8,128)}), f32[96,2]{1,0:T(8,128)}) %reduce-scatter.65.cloned.1.call-update) | async-done | bytes 784
  1364.2 63.3 %reduce-scatter.67.cloned.1.call-done = f32[96,2]{1,0:T(8,128)} async-done(((f32[768,2]{1,0:T(8,128)}), f32[96,2]{1,0:T(8,128)}) %reduce-scatter.67.cloned.1.call-update) | async-done | bytes 784
  1428.3 62.7 %reduce-scatter.69.cloned.1.call-done = f32[96,6]{1,0:T(8,128)} async-done(((f32[768,6]{1,0:T(8,128)}), f32[96,6]{1,0:T(8,128)}) %reduce-scatter.69.cloned.1.call-update) | async-done | bytes 2320
  1491.8 62.7 %reduce-scatter.71.cloned.1.call-done = f32[96,6]{1,0:T(8,128)} async-done(((f32[768,6]{1,0:T(8,128)}), f32[96,6]{1,0:T(8,128)}) %reduce-scatter.71.cloned.1.call-update) | async-done | bytes 2320
  1563.3 157.9 %reduce-scatter.53.cloned.1.call-done = f32[96,3072]{1,0:T(8,128)} async-done(((f32[768,3072]{1,0:T(8,128)}), f32[96,3072]{1,0:T(8,128)}) %reduce-scatter.53.cloned.1.call-update) | async-done | bytes 1179664 | tf_op jit(solution)/shard_map/reduce_scatter | solution.py:231
  1752.5 12.9 reduce-scatter.47.cloned.1.call-done
  1772.8 16.6 reduce-scatter.35.cloned.1.call-done
  1796.5 16.6 reduce-scatter.39.cloned.1.call-done
  1820.2 158.4 %reduce-scatter.61.cloned.1.call-done = f32[384,768]{1,0:T(8,128)} async-done(((f32[3072,768]{1,0:T(8,128)}), f32[384,768]{1,0:T(8,128)}) %reduce-scatter.61.cloned.1.call-update) | async-done | bytes 1179664 | tf_op jit(solution)/shard_map/reduce_scatter | solution.py:232
  1982.1 22.3 %reduce-scatter.51.cloned.1.call-done = bf16[24,3072]{1,0:T(8,128)(2,1)} async-done(((bf16[96,3072]{1,0:T(8,128)(2,1)}), bf16[24,3072]{1,0:T(8,128)(2,1)}) %reduce-scatter.51.cloned.1.call-update) | async-done | bytes 147472 | tf_op jit(solution)/shard_map/reduce_scatter | solution.py:244
  2012.2 16.6 reduce-scatter.59.cloned.1.call-done
  2036.6 17.2 reduce-scatter.55.cloned.1.call-done
  2063.2 15.2 reduce-scatter.63.cloned.1.call-done
  (507 shorter events, 370.3 us)
Async XLA Ops:
  7.2 198.3 %all-gather.27.cloned.1.call-start = ((), (), s32[]{:S(2)}) async-start(), calls=%async_computation.36 | async-start | bytes 3981312 | tf_op jit(solution)/shard_map/all_gather | solution.py:205
  9.5 206.1 %all-gather.29.cloned.1.call-start = ((), (), s32[]{:S(2)}) async-start(), calls=%async_computation.37 | async-start | bytes 1327104 | tf_op jit(solution)/shard_map/all_gather | solution.py:206
  11.3 207.5 %all-gather.35.cloned.1.call-start = ((), (), s32[]{:S(2)}) async-start(), calls=%async_computation.40 | async-start | bytes 3981312 | tf_op jit(solution)/shard_map/all_gather | solution.py:205
  12.1 243.6 %all-gather.37.cloned.1.call-start = ((), (), s32[]{:S(2)}) async-start(), calls=%async_computation.41 | async-start | bytes 1327104 | tf_op jit(solution)/shard_map/all_gather | solution.py:206
  12.6 306.3 %all-gather.31.cloned.1.call-start = ((), (), s32[]{:S(2)}) async-start(), calls=%async_computation.38 | async-start | bytes 5308416 | tf_op jit(solution)/shard_map/all_gather | solution.py:207
  13.8 385.8 %all-gather.33.cloned.1.call-start = ((), (), s32[]{:S(2)}) async-start(), calls=%async_computation.39 | async-start | bytes 5308416 | tf_op jit(solution)/shard_map/all_gather | solution.py:208
  15.0 465.4 %all-gather.39.cloned.1.call-start = ((), (), s32[]{:S(2)}) async-start(), calls=%async_computation.42 | async-start | bytes 5308416 | tf_op jit(solution)/shard_map/all_gather | solution.py:207
  15.8 544.9 %all-gather.41.cloned.1.call-start = ((), (), s32[]{:S(2)}) async-start(), calls=%async_computation.43 | async-start | bytes 5308416 | tf_op jit(solution)/shard_map/all_gather | solution.py:208
  16.5 665.1 %reduce-scatter.41.cloned.1.call-start = ((), (), s32[]{:S(2)}) async-start(), calls=%async_computation.24 | async-start | bytes 2654208 | tf_op jit(solution)/shard_map/reduce_scatter | solution.py:230
  16.7 188.7 %copy-start.70 = (f32[197]{0:T(256)}, f32[197]{0:T(256)S(1)}, u32[]{:S(2)}) copy-start(f32[197]{0:T(256)S(1)} %broadcast_multiply_fusion.3) | copy-start | bytes 2368
  17.0 188.5 %copy-start.67 = (f32[197]{0:T(256)}, f32[197]{0:T(256)S(1)}, u32[]{:S(2)}) copy-start(f32[197]{0:T(256)S(1)} %fusion.154) | copy-start | bytes 2368
  413.2 290.7 %reduce-scatter.45.cloned.1.call-start = ((), (), s32[]{:S(2)}) async-start(), calls=%async_computation.26 | async-start | bytes 2654208 | tf_op jit(solution)/shard_map/reduce_scatter | solution.py:230
  581.4 255.1 %reduce-scatter.33.cloned.1.call-start = ((), (), s32[]{:S(2)}) async-start(), calls=%async_computation.20 | async-start | bytes 7962624 | tf_op jit(solution)/shard_map/reduce_scatter | solution.py:229
  596.8 371.8 %reduce-scatter.37.cloned.1.call-start = ((), (), s32[]{:S(2)}) async-start(), calls=%async_computation.22 | async-start | bytes 7962624 | tf_op jit(solution)/shard_map/reduce_scatter | solution.py:229
  634.8 499.3 %reduce-scatter.49.cloned.1.call-start = ((), (), s32[]{:S(2)}) async-start(), calls=%async_computation.28 | async-start | bytes 10616832 | tf_op jit(solution)/shard_map/reduce_scatter | solution.py:231
  641.5 658.7 %reduce-scatter.57.cloned.1.call-start = ((), (), s32[]{:S(2)}) async-start(), calls=%async_computation.32 | async-start | bytes 10616832 | tf_op jit(solution)/shard_map/reduce_scatter | solution.py:232
  648.1 715.2 %reduce-scatter.65.cloned.1.call-start = ((), (), s32[]{:S(2)}) async-start(), calls=%async_computation.44 | async-start | bytes 442368
  664.1 763.3 %reduce-scatter.67.cloned.1.call-start = ((), (), s32[]{:S(2)}) async-start(), calls=%async_computation.45 | async-start | bytes 442368
  665.2 825.8 %reduce-scatter.69.cloned.1.call-start = ((), (), s32[]{:S(2)}) async-start(), calls=%async_computation.46 | async-start | bytes 442368
  669.6 885.0 %reduce-scatter.71.cloned.1.call-start = ((), (), s32[]{:S(2)}) async-start(), calls=%async_computation.47 | async-start | bytes 442368
  672.4 1048.7 %reduce-scatter.53.cloned.1.call-start = ((), (), s32[]{:S(2)}) async-start(), calls=%async_computation.30 | async-start | bytes 10616832 | tf_op jit(solution)/shard_map/reduce_scatter | solution.py:231
  681.5 289.1 %copy-start.35 = (bf16[1,512,768]{2,1,0:T(8,128)(2,1)S(1)}, bf16[1,512,768]{2,1,0:T(8,128)(2,1)}, u32[]{:S(2)}) copy-start(bf16[1,512,768]{2,1,0:T(8,128)(2,1)} %param.15) | copy-start | bytes 2359300
  681.5 1065.2 %reduce-scatter.43.cloned.1.call-start = ((), (), s32[]{:S(2)}) async-start(), calls=%async_computation.25 | async-start | bytes 184320 | tf_op jit(solution)/shard_map/reduce_scatter | solution.py:241
  683.3 1082.0 %reduce-scatter.47.cloned.1.call-start = ((), (), s32[]{:S(2)}) async-start(), calls=%async_computation.27 | async-start | bytes 184320 | tf_op jit(solution)/shard_map/reduce_scatter | solution.py:241
  705.6 1083.8 %reduce-scatter.35.cloned.1.call-start = ((), (), s32[]{:S(2)}) async-start(), calls=%async_computation.21 | async-start | bytes 552960 | tf_op jit(solution)/shard_map/reduce_scatter | solution.py:238
  838.5 974.6 %reduce-scatter.39.cloned.1.call-start = ((), (), s32[]{:S(2)}) async-start(), calls=%async_computation.23 | async-start | bytes 552960 | tf_op jit(solution)/shard_map/reduce_scatter | solution.py:238
  970.6 1008.0 %reduce-scatter.61.cloned.1.call-start = ((), (), s32[]{:S(2)}) async-start(), calls=%async_computation.34 | async-start | bytes 10616832 | tf_op jit(solution)/shard_map/reduce_scatter | solution.py:232
  978.9 1025.5 %reduce-scatter.51.cloned.1.call-start = ((), (), s32[]{:S(2)}) async-start(), calls=%async_computation.29 | async-start | bytes 737280 | tf_op jit(solution)/shard_map/reduce_scatter | solution.py:244
  1136.3 166.2 %copy-start.109 = (f32[768]{0:T(1024)S(1)}, f32[768]{0:T(1024)}, u32[]{:S(2)}) copy-start(f32[768]{0:T(1024)} %get-tuple-element.93) | copy-start | bytes 9220
  1136.3 892.5 %reduce-scatter.59.cloned.1.call-start = ((), (), s32[]{:S(2)}) async-start(), calls=%async_computation.33 | async-start | bytes 737280 | tf_op jit(solution)/shard_map/reduce_scatter | solution.py:247
  1302.5 751.4 %reduce-scatter.55.cloned.1.call-start = ((), (), s32[]{:S(2)}) async-start(), calls=%async_computation.31 | async-start | bytes 737280 | tf_op jit(solution)/shard_map/reduce_scatter | solution.py:244
  1723.3 355.1 %reduce-scatter.63.cloned.1.call-start = ((), (), s32[]{:S(2)}) async-start(), calls=%async_computation.35 | async-start | bytes 737280 | tf_op jit(solution)/shard_map/reduce_scatter | solution.py:247
  (122 other events, 1445.6 us)
Sparse Core Ops, SparseCore 0:
  10.8 65.6 all-gather.26
  79.3 43.0 all-gather.28
  125.1 71.3 all-gather.34
  199.1 39.1 all-gather.36
  240.9 78.0 all-gather.30
  321.6 78.0 all-gather.32
  402.4 78.0 all-gather.38
  482.6 78.0 all-gather.40
  564.8 67.2 reduce-scatter.40
  636.0 67.9 reduce-scatter.44
  707.6 128.7 reduce-scatter.32
  840.5 128.0 reduce-scatter.36
  972.1 161.9 reduce-scatter.48
  1137.6 162.6 reduce-scatter.56
  1303.4 59.8 reduce-scatter.64
  1367.0 60.3 reduce-scatter.66
  1430.5 60.3 reduce-scatter.68
  1494.1 60.3 reduce-scatter.70
  1558.1 162.9 reduce-scatter.52
  1723.4 19.7 reduce-scatter.42
  1745.7 19.6 reduce-scatter.46
  1767.8 21.5 reduce-scatter.34
  1792.0 21.1 reduce-scatter.38
  1816.6 161.9 reduce-scatter.60
  1981.7 22.6 reduce-scatter.50
  2006.7 22.0 reduce-scatter.58
  2031.7 22.0 reduce-scatter.54
  2056.3 22.0 reduce-scatter.62
where the time goes:
time: 2100 us; the launch traced here: 2090 us
  waiting for transfers between devices  1480 us (70%)
  blocking collectives  274 us (13%)
  matrix products  170 us (8%)
  other arithmetic  97.4 us (5%)
  local copies, waits for them, and re-layouts  48.3 us (2%)
    reduce_scatter x2, waiting for transfers between devices, reduce_grads(): lax.psum_scatter(gradients[2], 'fsdp', scatter_dimension=0, tiled=True)  313 us
    reduce_scatter x2, waiting for transfers between devices, reduce_grads(): lax.psum_scatter(gradients[3], 'fsdp', scatter_dimension=0, tiled=True)  275 us
    reduce_scatter x2, waiting for transfers between devices, reduce_grads(): lax.psum_scatter(gradients[0], 'fsdp', scatter_dimension=0, tiled=True)  261 us
    unnamed x32, waiting for transfers between devices  242 us
    all_gather x2, waiting for transfers between devices, fetch_weights(): lax.all_gather(w_down[layer_index], 'fsdp', axis=0, tiled=True)  130 us
    all_gather x2, waiting for transfers between devices, fetch_weights(): lax.all_gather(w_up[layer_index], 'fsdp', axis=0, tiled=True)  125 us
    all_gather x2, blocking collectives, fetch_weights(): lax.all_gather(biases[layer_index], 'fsdp', axis=1, tiled=True)  53.2 us
    all_gather x2, blocking collectives, fetch_weights(): lax.all_gather(gains[layer_index], 'fsdp', axis=1, tiled=True)  49.3 us
  transfers between devices with their start and end apart: 28, of which 22 were waited for; matrix products, arithmetic and copies ran while one was open for 14% of the time, Pallas kernels for 0%

commit v1 on v0

--- a/solution.py
+++ b/solution.py
@@ -1,10 +1,492 @@
+import functools
+
 import jax
 import jax.numpy as jnp
 from jax import lax
+from jax.experimental import pallas as pl
+from jax.experimental.pallas import tpu as pltpu
 from jax.sharding import PartitionSpec as P
 
 HEAD = 64
 
+MESH = pl.DeviceIdType.MESH
+UP, DOWN, YWAY, XWAY, CORE, COREY, COREX = range(7)
+
+
+class Place:
+    def __init__(self, line):
+        dp, fs = lax.axis_index("dp"), lax.axis_index("fsdp")
+        self.line = line
+        self.dp, self.fs = dp, fs
+        self.x, self.c = dp // 2, dp % 2
+        self.z, self.y = fs // 2, fs % 2
+        self.up = (dp, fs + 2)
+        self.down = (dp, fs - 2)
+        self.yway = (dp, self.z * 2 + 1 - self.y)
+        self.xway = ((1 - self.x) * 2 + self.c, fs)
+        self.core = (self.x * 2 + 1 - self.c, fs)
+        self.has_up = self.z + 1 < line
+        self.has_down = self.z > 0
+
+    def greet(self):
+        barrier = pltpu.get_barrier_semaphore()
+        total = 0
+        for step in range(1, 2 * self.line):
+            other = lax.rem(self.fs + step, 2 * self.line)
+            pl.semaphore_signal(barrier, inc=1, device_id=(self.dp, other), device_id_type=MESH)
+            total += 1
+        for step in range(1, 4):
+            other = lax.rem(self.dp + step, 4)
+            pl.semaphore_signal(barrier, inc=1, device_id=(other, self.fs), device_id_type=MESH)
+            total += 1
+        pl.semaphore_wait(barrier, total)
+
+
+def remote(src, dst, send, recv, device):
+    return pltpu.make_async_remote_copy(
+        src_ref=src, dst_ref=dst, send_sem=send, recv_sem=recv, device_id=device, device_id_type=MESH
+    )
+
+
+class Gather:
+    def __init__(self, at, place, own, full, send, recv, near):
+        self.at, self.place, self.own, self.full = at, place, own, full
+        self.send, self.recv, self.near = send, recv, near
+        self.rows = own.shape[0]
+        self.deep = self.rows // 2
+        self.half = own.shape[1] // 2
+
+    def rows_of(self, block, y, c):
+        start = (block * 2 + y) * self.rows + c * self.deep
+        return pl.ds(pl.multiple_of(start, 16), self.deep)
+
+    def cols_of(self, x):
+        return pl.ds(pl.multiple_of(x * self.half, 128), self.half)
+
+    def copy(self, kind, block):
+        p, s, r = self.place, self.send.at[self.at, kind, block], None
+        if kind in (UP, DOWN):
+            ref = self.full.at[self.rows_of(block, p.y, p.c)]
+            return remote(ref, ref, s, self.recv.at[self.at, UP, block], p.up if kind == UP else p.down)
+        if kind == YWAY:
+            ref = self.full.at[self.rows_of(block, p.y, p.c), self.cols_of(p.x)]
+            return remote(ref, ref, s, self.recv.at[self.at, kind, block], p.yway)
+        if kind == XWAY:
+            ref = self.full.at[self.rows_of(block, 1 - p.y, p.c), self.cols_of(p.x)]
+            return remote(ref, ref, s, self.recv.at[self.at, kind, block], p.xway)
+        if kind == CORE:
+            ref = self.full.at[self.rows_of(block, p.y, p.c)]
+        elif kind == COREY:
+            ref = self.full.at[self.rows_of(block, 1 - p.y, p.c), self.cols_of(p.x)]
+        else:
+            ref = self.full.at[self.rows_of(block, 1 - p.y, p.c), self.cols_of(1 - p.x)]
+        return remote(ref, ref, s, self.recv.at[self.at, kind, block], p.core)
+
+    def landed(self, kind, block):
+        p, s = self.place, self.send.at[self.at, kind, block]
+        r = self.recv.at[self.at, kind, block]
+        if kind == UP:
+            ref = self.full.at[self.rows_of(block, p.y, p.c)]
+        elif kind == YWAY:
+            ref = self.full.at[self.rows_of(block, 1 - p.y, p.c), self.cols_of(p.x)]
+        elif kind == XWAY:
+            ref = self.full.at[self.rows_of(block, 1 - p.y, p.c), self.cols_of(1 - p.x)]
+        elif kind == CORE:
+            ref = self.full.at[self.rows_of(block, p.y, 1 - p.c)]
+        elif kind == COREY:
+            ref = self.full.at[self.rows_of(block, 1 - p.y, 1 - p.c), self.cols_of(p.x)]
+        else:
+            ref = self.full.at[self.rows_of(block, 1 - p.y, 1 - p.c), self.cols_of(1 - p.x)]
+        return remote(ref, ref, s, r, p.core)
+
+    def own_copy(self):
+        start = pl.multiple_of(self.place.fs * self.rows, 16)
+        return pltpu.make_async_copy(self.own, self.full.at[pl.ds(start, self.rows)], self.near.at[self.at])
+
+    def first(self):
+        p = self.place
+        self.own_copy().start()
+        mine = self.own.at[pl.ds(pl.multiple_of(p.c * self.deep, 16), self.deep)]
+        there = self.full.at[self.rows_of(p.z, p.y, p.c)]
+
+        def out(kind, device):
+            return remote(mine, there, self.send.at[self.at, kind, p.z], self.recv.at[self.at, UP, p.z], device)
+
+        pl.when(p.has_up)(lambda: out(UP, p.up).start())
+        pl.when(p.has_down)(lambda: out(DOWN, p.down).start())
+        cols = self.cols_of(p.x)
+        remote(
+            mine.at[:, cols],
+            there.at[:, cols],
+            self.send.at[self.at, YWAY, p.z],
+            self.recv.at[self.at, YWAY, p.z],
+            p.yway,
+        ).start()
+
+    def line_step(self, k):
+        p = self.place
+
+        def pass_on(block, kind, more):
+            self.landed(UP, block).wait_recv()
+            pl.when(more)(lambda: self.copy(kind, block).start())
+            self.copy(YWAY, block).start()
+            self.copy(CORE, block).start()
+
+        pl.when(p.z - k >= 0)(lambda: pass_on(p.z - k, UP, p.has_up))
+        pl.when(p.z + k < p.line)(lambda: pass_on(p.z + k, DOWN, p.has_down))
+
+    def near_blocks(self, k, body):
+        p = self.place
+        if k == 0:
+            body(p.z)
+            return
+        pl.when(p.z - k >= 0)(lambda: body(p.z - k))
+        pl.when(p.z + k < p.line)(lambda: body(p.z + k))
+
+    def y_step(self, k):
+        def body(block):
+            self.landed(YWAY, block).wait_recv()
+            self.copy(XWAY, block).start()
+            self.copy(COREY, block).start()
+
+        self.near_blocks(k, body)
+
+    def x_step(self, k):
+        def body(block):
+            self.landed(XWAY, block).wait_recv()
+            self.copy(COREX, block).start()
+
+        self.near_blocks(k, body)
+
+    def stage(self, j):
+        line = self.place.line
+        if j == 0:
+            self.first()
+        if 1 <= j < line:
+            self.line_step(j)
+        if 1 <= j <= line:
+            self.y_step(j - 1)
+        if 2 <= j <= line + 1:
+            self.x_step(j - 2)
+
+    def arrive(self):
+        p = self.place
+        self.own_copy().wait()
+
+        def body(block, carry):
+            pl.when(block != p.z)(lambda: self.landed(CORE, block).wait_recv())
+            self.landed(COREY, block).wait_recv()
+            self.landed(COREX, block).wait_recv()
+            return carry
+
+        lax.fori_loop(0, p.line, body, 0)
+
+    def drain(self):
+        p = self.place
+
+        def body(block, carry):
+            pl.when(p.has_up & (block <= p.z))(lambda: self.copy(UP, block).wait_send())
+            pl.when(p.has_down & (block >= p.z))(lambda: self.copy(DOWN, block).wait_send())
+            pl.when(block != p.z)(lambda: self.copy(CORE, block).wait_send())
+            for kind in (YWAY, XWAY, COREY, COREX):
+                self.copy(kind, block).wait_send()
+            return carry
+
+        lax.fori_loop(0, p.line, body, 0)
+
+
+GATHER_STAGES = 2
+
+
+def gather_kernel(line, order, *refs):
+    owned, small, fulls, small_all = refs[:4], refs[4], refs[5:13], refs[13]
+    send, recv, near, small_send, small_recv = refs[14:]
+    place = Place(line)
+    place.greet()
+    smalls = []
+    for step in range(1, 2 * line):
+        other = lax.rem(place.fs + step, 2 * line)
+        smalls.append(
+            remote(small, small_all.at[place.fs], small_send.at[step], small_recv.at[place.fs], (place.dp, other))
+        )
+        smalls[-1].start()
+    kept = pltpu.make_async_copy(small, small_all.at[place.fs], small_send.at[0])
+    kept.start()
+    units = [
+        Gather(at, place, owned[which].at[layer], fulls[layer * 4 + which], send, recv, near)
+        for at, (layer, which) in enumerate(order)
+    ]
+    stages = line + GATHER_STAGES
+    for slot in range(len(units) + stages - 1):
+        for j in range(stages):
+            if 0 <= slot - j < len(units):
+                units[slot - j].stage(j)
+    for unit in units:
+        unit.arrive()
+    for unit in units:
+        unit.drain()
+    kept.wait()
+    for step in range(1, 2 * line):
+        other = lax.rem(place.fs + step, 2 * line)
+        smalls[step - 1].wait_send()
+        remote(
+            small, small_all.at[other], small_send.at[step], small_recv.at[other], (place.dp, other)
+        ).wait_recv()
+
+
+def gather_all(line, owned, small):
+    width = [ref.shape for ref in owned]
+    outs = [
+        jax.ShapeDtypeStruct((2 * line * width[which][1], width[which][2]), owned[which].dtype)
+        for layer in range(2)
+        for which in range(4)
+    ]
+    outs.append(jax.ShapeDtypeStruct((2 * line, *small.shape), small.dtype))
+    order = [(layer, which) for layer in range(2) for which in range(4)]
+    anywhere = pl.BlockSpec(memory_space=pl.ANY)
+    return pl.pallas_call(
+        functools.partial(gather_kernel, line, order),
+        out_shape=outs,
+        in_specs=[anywhere] * 5,
+        out_specs=[anywhere] * 9,
+        scratch_shapes=[
+            pltpu.SemaphoreType.DMA((8, 7, line)),
+            pltpu.SemaphoreType.DMA((8, 7, line)),
+            pltpu.SemaphoreType.DMA((8,)),
+            pltpu.SemaphoreType.DMA((2 * line,)),
+            pltpu.SemaphoreType.DMA((2 * line,)),
+        ],
+        compiler_params=pltpu.CompilerParams(collective_id=0, has_side_effects=True),
+    )(*owned, small)
+
+
+class Reduce:
+    def __init__(self, at, place, terms, out, bufs, send, recv, near):
+        self.at, self.place, self.terms, self.out = at, place, terms, out
+        self.mine, self.other, self.from_x, self.from_y, self.line_in, self.last_x, self.total = bufs
+        self.send, self.recv, self.near = send, recv, near
+        self.deep, self.half = self.mine.shape[2], self.mine.shape[3] // 2
+
+    def cols_of(self, x):
+        return pl.ds(pl.multiple_of(x * self.half, 128), self.half)
+
+    def sems(self, kind, block=0):
+        return self.send.at[self.at, kind, block], self.recv.at[self.at, kind, block]
+
+    def core_copy(self):
+        p = self.place
+        return remote(self.terms.at[:, :, 1 - p.c], self.other, *self.sems(0), p.core)
+
+    def near_copy(self):
+        return pltpu.make_async_copy(self.terms.at[:, :, self.place.c], self.mine, self.near.at[self.at])
+
+    def x_copy(self):
+        p = self.place
+        return remote(self.mine.at[:, 1 - p.y, :, self.cols_of(1 - p.x)], self.from_x, *self.sems(1), p.xway)
+
+    def y_copy(self):
+        p = self.place
+        return remote(self.mine.at[:, 1 - p.y, :, self.cols_of(p.x)], self.from_y, *self.sems(2), p.yway)
+
+    def line_copy(self, way, block):
+        p = self.place
+        return remote(
+            self.mine.at[block, p.y], self.line_in.at[way, block], *self.sems(3 + way, block), (p.up, p.down)[way]
+        )
+
+    def last_copy(self):
+        p = self.place
+        return remote(self.mine.at[p.z, p.y], self.last_x, *self.sems(5), p.xway)
+
+    def out_rows(self, c):
+        return self.out.at[pl.ds(pl.multiple_of(c * self.deep, 8), self.deep)]
+
+    def out_copy(self):
+        return remote(self.total, self.out_rows(self.place.c), *self.sems(6), self.place.core)
+
+    def out_near(self):
+        return pltpu.make_async_copy(self.total, self.out_rows(self.place.c), self.near.at[self.at])
+
+    def start(self):
+        self.core_copy().start()
+        self.near_copy().start()
+
+    def add_core(self):
+        self.near_copy().wait()
+        self.core_copy().wait_recv()
+        lines = self.mine.shape[0]
+
+        def body(at, carry):
+            block, y = at // 2, at % 2
+            self.mine[block, y] = self.mine[block, y] + self.other[block, y]
+            return carry
+
+        lax.fori_loop(0, 2 * lines, body, 0)
+        self.x_copy().start()
+
+    def add_x(self):
+        p = self.place
+        self.x_copy().wait_recv()
+        cols = self.cols_of(p.x)
+
+        def body(block, carry):
+            self.mine[block, 1 - p.y, :, cols] = self.mine[block, 1 - p.y, :, cols] + self.from_x[block]
+            return carry
+
+        lax.fori_loop(0, self.mine.shape[0], body, 0)
+        self.y_copy().start()
+
+    def add_y(self):
+        p = self.place
+        self.y_copy().wait_recv()
+        cols = self.cols_of(p.x)
+
+        def body(block, carry):
+            self.mine[block, p.y, :, cols] = self.mine[block, p.y, :, cols] + self.from_y[block]
+            return carry
+
+        lax.fori_loop(0, self.mine.shape[0], body, 0)
+
+    def add_line(self, way, block):
+        p = self.place
+        self.line_copy(way, block).wait_recv()
+        self.mine[block, p.y] = self.mine[block, p.y] + self.line_in[way, block]
+
+    def line_step(self, k):
+        p, line = self.place, self.place.line
+        far = line - 1 - k
+        for way, block, valid, more in (
+            (0, far, far > p.z, p.has_down),
+            (1, k, k < p.z, p.has_up),
+        ):
+
+            def body(way=way, block=block, more=more):
+                pl.when(more)(lambda: self.add_line(way, block))
+                self.line_copy(way, block).start()
+
+            pl.when(valid)(body)
+
+    def own_step(self):
+        p = self.place
+        pl.when(p.has_down)(lambda: self.add_line(0, p.z))
+        pl.when(p.has_up)(lambda: self.add_line(1, p.z))
+        self.last_copy().start()
+
+    def finish(self):
+        p = self.place
+        self.last_copy().wait_recv()
+        self.total[...] = self.mine[p.z, p.y].astype(jnp.float32) + self.last_x[...].astype(jnp.float32)
+        self.out_copy().start()
+        self.out_near().start()
+
+    def stages(self):
+        line = self.place.line
+        steps = [self.start, self.add_core, self.add_x, self.add_y]
+        steps += [functools.partial(self.line_step, k) for k in range(line - 1)]
+        return steps + [self.own_step, self.finish]
+
+    def drain(self):
+        p = self.place
+        self.core_copy().wait_send()
+        self.x_copy().wait_send()
+        self.y_copy().wait_send()
+        for block in range(p.line):
+            pl.when(block > p.z)(lambda: self.line_copy(0, block).wait_send())
+            pl.when(block < p.z)(lambda: self.line_copy(1, block).wait_send())
+        self.last_copy().wait_send()
+        self.out_copy().wait()
+        self.out_near().wait()
+
+
+def reduce_kernel(line, order, *refs):
+    terms, small, outs, small_out = refs[:8], refs[8], refs[9:13], refs[13]
+    bufs, refs = refs[14 : 14 + 7 * 8], refs[14 + 7 * 8 :]
+    small_in, small_sum, small_four, send, recv, near, small_send, small_recv = refs
+    place = Place(line)
+    place.greet()
+    fs, dp, n = place.fs, place.dp, 2 * line
+    for step in range(1, n):
+        other = lax.rem(fs + step, n)
+        remote(small.at[other], small_in.at[fs], small_send.at[0, other], small_recv.at[0, fs], (dp, other)).start()
+    kept = pltpu.make_async_copy(small.at[fs], small_in.at[fs], small_send.at[0, fs])
+    kept.start()
+    units = [
+        Reduce(at, place, terms[layer * 4 + which], outs[which].at[layer], bufs[7 * at : 7 * at + 7], send, recv, near)
+        for at, (layer, which) in enumerate(order)
+    ]
+    steps = [unit.stages() for unit in units]
+    deep = len(steps[0])
+    for slot in range(len(units) + deep - 1):
+        if slot == 2:
+            kept.wait()
+            for step in range(1, n):
+                other = lax.rem(fs + step, n)
+                remote(
+                    small.at[other], small_in.at[other], small_send.at[0, other], small_recv.at[0, other], (dp, other)
+                ).wait()
+            small_sum[...] = jnp.sum(small_in[...], axis=0)
+            small_four[dp] = small_sum[...]
+            for step in range(1, 4):
+                other = lax.rem(dp + step, 4)
+                remote(
+                    small_sum, small_four.at[dp], small_send.at[1, other], small_recv.at[1, dp], (other, fs)
+                ).start()
+        if slot == 4:
+            for step in range(1, 4):
+                other = lax.rem(dp + step, 4)
+                remote(
+                    small_sum, small_four.at[other], small_send.at[1, other], small_recv.at[1, other], (other, fs)
+                ).wait()
+            small_out[...] = jnp.sum(small_four[...], axis=0)
+        for j in range(deep):
+            if 0 <= slot - j < len(units):
+                steps[slot - j][j]()
+    for unit in units:
+        unit.drain()
+
+
+def reduce_all(line, terms, small):
+    order = [(layer, which) for layer in range(2) for which in (3, 2, 1, 0)]
+    split, bufs = [], []
+    for term in terms:
+        deep = term.shape[0] // (4 * line)
+        split.append(term.reshape(line, 2, 2, deep, term.shape[1]))
+    for layer, which in order:
+        _, _, _, deep, width = split[layer * 4 + which].shape
+        low = jnp.bfloat16
+        bufs += [
+            pltpu.VMEM((line, 2, deep, width), low),
+            pltpu.VMEM((line, 2, deep, width), low),
+            pltpu.VMEM((line, deep, width // 2), low),
+            pltpu.VMEM((line, deep, width // 2), low),
+            pltpu.VMEM((2, line, deep, width), low),
+            pltpu.VMEM((deep, width), low),
+            pltpu.VMEM((deep, width), jnp.float32),
+        ]
+    outs = [
+        jax.ShapeDtypeStruct((2, split[which].shape[3] * 2, split[which].shape[4]), jnp.float32) for which in range(4)
+    ]
+    outs.append(jax.ShapeDtypeStruct(small.shape[1:], jnp.float32))
+    anywhere = pl.BlockSpec(memory_space=pl.ANY)
+    inside = pl.BlockSpec(memory_space=pltpu.VMEM)
+    return pl.pallas_call(
+        functools.partial(reduce_kernel, line, order),
+        out_shape=outs,
+        in_specs=[anywhere] * 8 + [inside],
+        out_specs=[anywhere] * 4 + [inside],
+        scratch_shapes=bufs
+        + [
+            pltpu.VMEM(small.shape, jnp.float32),
+            pltpu.VMEM(small.shape[1:], jnp.float32),
+            pltpu.VMEM((4, *small.shape[1:]), jnp.float32),
+            pltpu.SemaphoreType.DMA((8, 7, line)),
+            pltpu.SemaphoreType.DMA((8, 7, line)),
+            pltpu.SemaphoreType.DMA((8,)),
+            pltpu.SemaphoreType.DMA((2, 2 * line)),
+            pltpu.SemaphoreType.DMA((2, 2 * line)),
+        ],
+        compiler_params=pltpu.CompilerParams(collective_id=1, has_side_effects=True, vmem_limit_bytes=62 * 2**20),
+    )(*split, small)
 
 def normed(values, gain, shift):
     center = values - jnp.mean(values, axis=-1, keepdims=True)
@@ -195,6 +677,7 @@
         ]
     )
     return (
+        result.astype(jnp.bfloat16),
         grad_inputs,
         (grad_qkvw, grad_outw, grad_upw, grad_downw, grad_gains, grad_biases, grad_upb),
     )
@@ -282,7 +765,7 @@
     )
 
 
-def local(
+def plain(
     images,
     image_cot,
     captions,
@@ -304,13 +787,65 @@
     second_weights = fetch_weights(1, *owned)
     caption_out = forward_layer(captions, second_weights, caption_seg)[-1].astype(jnp.bfloat16)
     second_back = fetch_again(1, *owned)
-    caption_grad, caption_terms = backward_layer(captions, caption_cot, second_back, caption_seg)
+    _, caption_grad, caption_terms = backward_layer(captions, caption_cot, second_back, caption_seg)
     caption_shares = reduce_grads(caption_terms)
     first_back = fetch_again(0, *owned)
-    image_grad, image_terms = backward_layer(images, image_cot, first_back, image_seg)
+    _, image_grad, image_terms = backward_layer(images, image_cot, first_back, image_seg)
     image_shares = reduce_grads(image_terms)
     stacked = tuple((jnp.stack([image_shares[index], caption_shares[index]]) for index in range(7)))
     return (image_out, caption_out, image_grad, caption_grad) + stacked
+
+
+def kernels_fit(mesh, w_qkv):
+    return mesh.shape["dp"] == 4 and mesh.shape["fsdp"] % 2 == 0 and w_qkv.shape[1] % 32 == 0
+
+
+def pack_small(gains, biases, b_up):
+    rows = jnp.concatenate([gains.reshape(2, -1), biases.reshape(2, -1), b_up], axis=1).astype(jnp.float32).reshape(-1)
+    return jnp.pad(rows, (0, -rows.size % 1024)).reshape(-1, 128)
+
+
+def unpack_small(blocks, width, deep):
+    count = blocks.shape[0]
+    flat = blocks.reshape(count, -1)[:, : 2 * (8 * width + deep)].reshape(count, 2, 8 * width + deep)
+    rows = flat[:, :, : 8 * width].reshape(count, 2, 8, width).transpose(1, 2, 0, 3).reshape(2, 8, count * width)
+    up = flat[:, :, 8 * width :].transpose(1, 0, 2).reshape(2, count * deep)
+    return rows[:, :2], rows[:, 2:], up
+
+
+def spread_small(count, gains, biases, b_up):
+    rows = jnp.concatenate([gains, biases], axis=1)
+    width, deep = rows.shape[2] // count, b_up.shape[1] // count
+    rows = rows.reshape(2, 8, count, width).transpose(2, 0, 1, 3).reshape(count, 2, 8 * width)
+    up = b_up.reshape(2, count, deep).transpose(1, 0, 2)
+    flat = jnp.concatenate([rows, up], axis=2).reshape(count, -1)
+    return jnp.pad(flat, ((0, 0), (0, -flat.shape[1] % 1024))).reshape(count, -1, 128)
+
+
+def local(mesh, images, image_cot, captions, caption_cot, lengths, w_qkv, w_out, w_up, w_down, gains, biases, b_up):
+    if not kernels_fit(mesh, w_qkv):
+        return plain(
+            images, image_cot, captions, caption_cot, lengths, w_qkv, w_out, w_up, w_down, gains, biases, b_up
+        )
+    count = mesh.shape["fsdp"]
+    line = count // 2
+    width, deep = gains.shape[2], b_up.shape[1]
+    *fulls, small = gather_all(line, (w_qkv, w_out, w_up, w_down), pack_small(gains, biases, b_up))
+    gains_all, biases_all, up_all = unpack_small(small, width, deep)
+    outs, grads, terms, smalls = [], [], [], []
+    image_seg = jnp.zeros((images.shape[0], images.shape[1]), jnp.int32)
+    caption_seg = segment_ids(lengths, captions.shape[1])
+    for layer, (rows, cot, seg) in enumerate(((images, image_cot, image_seg), (captions, caption_cot, caption_seg))):
+        weights = (*fulls[layer * 4 : layer * 4 + 4], gains_all[layer], biases_all[layer], up_all[layer])
+        result, grad, found = backward_layer(rows, cot, weights, seg)
+        outs.append(result)
+        grads.append(grad)
+        terms += [term.astype(jnp.bfloat16) for term in found[:4]]
+        smalls.append(found[4:])
+    packed = spread_small(count, *(jnp.stack([smalls[0][at], smalls[1][at]]) for at in range(3)))
+    *shares, small_share = reduce_all(line, terms, packed)
+    rest = unpack_small(small_share[None], width, deep)
+    return (*outs, *grads, *shares, *rest)
 
 
 def solution(mesh):
@@ -329,7 +864,7 @@
         P(None, "fsdp"),
     )
     return jax.shard_map(
-        local,
+        functools.partial(local, mesh),
         mesh=mesh,
         in_specs=placed,
         out_specs=(

time: 2100 us -> 569 us (0.27)
  waiting for transfers between devices: 1480 us -> 0 us
  Pallas kernels: 0 us -> 345 us
  blocking collectives: 274 us -> 0 us
  other arithmetic: 97.4 us -> 38 us
  matrix products: 170 us -> 130 us
    reduce_scatter x16 -> x0, waiting for transfers between devices: 987 us -> none  [the longest x2 313 us: reduce_grads(): lax.psum_scatter(gradients[2], 'fsdp', scatter_dimension=0, tiled=True)]
    pallas_call x0 -> x2, Pallas kernels: none -> 345 us  [the longest x1 223 us: reduce_all(): pl.pallas_call(functools.partial(reduce_kernel, line, order), out_shape=o...]
    all_gather x8 -> x0, waiting for transfers between devices: 255 us -> none  [the longest x2 130 us: fetch_weights(): lax.all_gather(w_down[layer_index], 'fsdp', axis=0, tiled=True)]
    unnamed x32 -> x0, waiting for transfers between devices: 242 us -> none
    all_gather x18 -> x0, blocking collectives: 225 us -> none  [the longest x2 53.2 us: fetch_weights(): lax.all_gather(biases[layer_index], 'fsdp', axis=1, tiled=True)]
    convert_element_type x14 -> x0, other arithmetic: 55 us -> none  [the longest x2 28 us: forward_layer(): hidden + jnp.einsum('blf,fd->bld', activated, down_weight, preferred_elem...]
    unnamed x3 -> x0, blocking collectives: 49 us -> none
  transfers between devices with their start and end apart: 28 -> 0, of which waited for: 22 -> 0; matrix products, arithmetic and copies ran while one was open for 14% -> 0% of each run, Pallas kernels for 0% -> 0%
where the time goes in v1:
time: 569 us; the launch traced here: 564 us
  Pallas kernels  345 us (61%)
  matrix products  130 us (23%)
  local copies, waits for them, and re-layouts  48.2 us (8%)
  other arithmetic  38 us (7%)
    pallas_call x1, Pallas kernels, reduce_all(): pl.pallas_call(functools.partial(reduce_kernel, line, order), out_shape=o...  223 us
    pallas_call x1, Pallas kernels, gather_all(): pl.pallas_call(functools.partial(gather_kernel, line, order), out_shape=o...  122 us
    dot_general x2, matrix products, forward_layer(): jnp.einsum('bld,df->blf', normed_c, up_weight, preferred_element_type=jnp...  28.4 us
    unnamed x264, local copies, waits for them, and re-layouts  23.8 us
    dot_general x2, matrix products, backward_layer(): jnp.einsum('bld,fd->blf', cotangent, down_weight, preferred_element_type=...  13.7 us

profile of v1, /device:TPU:9, one launch (start us, length us, event | category | flops | bytes accessed | tf_op | source)
XLA Modules:
  0.0 563.7 jit_solution(12883715468005691465)
XLA Ops:
  12.3 121.6 %shard_map.203 = (bf16[768,2304]{1,0:T(8,128)(2,1)}, bf16[768,768]{1,0:T(8,128)(2,1)}, bf16[768,3072]{1,0:T(8,128)(2,1)}, bf16[3072,768]{1,0:T(8,128)(2,1)}, bf1...) custom-call(bf16[2,96,2304]{2,1,0:T(8,128)(2,1)} %refs_0_.1, ...), custom_call_target="tpu_custom_call" | custom-call | tf_op jit(solution)/shard_map/pallas_call | solution.py:247
  137.0 3.0 convolution_bitcast_fusion.2
  148.1 2.2 convolution_bitcast_fusion
  152.6 2.3 copy.96
  154.9 2.3 copy.97
  157.2 2.3 copy.95
  159.5 8.3 %multiply_convert_fusion.3 = (bf16[197,3072]{1,0:T(8,128)(2,1)S(1)}, f32[197,3072]{1,0:T(8,128)S(1)}, f32[197,3072]{1,0:T(8,128)S(1)}) fusion(f32[3072]{0:T(1024)} %add.252, bf16[768,3072]{1,0:T(8,128)(2,1)} %get-tuple-element.28, f32[1,197,768]{2,1,0:T(8,128)} %get-tuple-element.136, f32[768]{0:T(1024)} %get-tuple-element.100, ...), kind=kOutput, calls=%fused_computation.55 | convolution fusion | flops 970261248 | bytes 11395624 | tf_op jit(solution)/shard_map/bld,df->blf/dot_general | solution.py:585
  167.8 5.4 convert_reduce_fusion.2
  173.3 4.8 fusion.60
  178.1 5.6 fusion.86
  210.9 3.1 convolution_convert_fusion.5
  214.0 5.3 convolution_convert_fusion.1
  219.3 3.7 convolution_convert_fusion
  225.0 2.2 fusion
  227.2 2.3 copy-done
  229.5 3.2 fusion.52
  234.2 20.1 %multiply_convert_fusion.1 = (bf16[512,3072]{1,0:T(8,128)(2,1)S(1)}, f32[512,3072]{1,0:T(8,128)S(1)}, f32[512,3072]{1,0:T(8,128)}) fusion(f32[3072]{0:T(1024)S(1)} %copy-done.97, bf16[768,3072]{1,0:T(8,128)(2,1)} %get-tuple-element.32, f32[1,512,768]{2,1,0:T(8,128)S(1)} %get-tuple-element.141, f32[768]{0:T(1024)S(1)} %copy-done.107, ...), kind=kOutput, calls=%fused_computation.20 | convolution fusion | flops 2521694208 | bytes 22042624 | tf_op jit(solution)/shard_map/bld,df->blf/dot_general | solution.py:585
  254.4 8.2 %convert_reduce_fusion = (f32[3072]{0:T(1024)S(1)}, bf16[512,3072]{1,0:T(8,128)(2,1)S(1)}) fusion(f32[512,3072]{1,0:T(8,128)S(1)} %get-tuple-element.116, bf16[3072,768]{1,0:T(8,128)(2,1)S(1)} %bitcast.352, bf16[1,512,768]{2,1,0:T(8,128)(2,1)S(1)} %copy-done.32, f32[512,3072]{1,0:T(8,128)} %get-tuple-element.142, f32[3072]{0:T(1024)S(1)} %copy-done.97), kind=kOutput, calls=%fused_computation.19 | convolution fusion | flops 2442654720 | bytes 21258240 | tf_op jit(solution)/shard_map/bld,fd->blf/dot_general | solution.py:628
  262.6 3.5 fusion.48
  266.2 2.9 fusion.45
  270.2 2.6 fusion.115
  273.5 4.8 convolution_convert_fusion.3
  282.7 3.4 convolution_convert_fusion.6
  286.2 7.3 %fusion.49 = bf16[12,64,512]{2,1,0:T(8,128)(2,1)} fusion(bf16[512,12,64]{0,2,1:T(8,128)(2,1)S(1)} %bitcast.315, f32[12,512,512]{1,2,0:T(8,128)} %copy-done, f32[12,512]{1,0:T(8,128)S(1)} %log_add_fusion, pred[512,512]{0,1:T(8,128)(4,1)S(1)} %copy-done.9), kind=kOutput, calls=%fused_computation.117 | convolution fusion | flops 415629312 | bytes 14442496 | tf_op jit(solution)/shard_map/bhqk,bqhd->bkhd/dot_general | solution.py:554
  293.6 4.4 convolution_convert_fusion.2
  298.0 7.0 %multiply_reduce_fusion = (f32[12,512]{1,0:T(8,128)S(1)}, f32[12,512,512]{1,2,0:T(8,128)}) fusion(f32[12,512,512]{1,2,0:T(8,128)S(1)} %bitcast.292, f32[12,512]{1,0:T(8,128)S(1)} %log_add_fusion, pred[512,512]{0,1:T(8,128)(4,1)S(1)} %copy-done.9, bf16[512,12,64]{0,2,1:T(8,128)(2,1)S(1)} %bitcast.316, bf16[512,12,64]{0,2,1:T(8,128)(2,1)S(1)} %bitcast.314), kind=kOutput, calls=%fused_computation.1 | convolution fusion | flops 418375680 | bytes 27049984 | tf_op jit(solution)/shard_map/bqhd,bkhd->bhqk/dot_general | solution.py:543
  304.9 7.2 %multiply_convert_fusion = bf16[12,512,512]{1,2,0:T(8,128)(2,1)S(1)} fusion(f32[12,512,512]{1,2,0:T(8,128)} %get-tuple-element.150, f32[12,512,512]{1,2,0:T(8,128)S(1)} %bitcast.292, f32[12,512]{1,0:T(8,128)S(1)} %get-tuple-element.149, f32[12,512]{1,0:T(8,128)S(1)} %log_add_fusion, pred[512,512]{0,1:T(8,128)(4,1)S(1)} %copy-done.9), kind=kLoop, calls=%fused_computation | loop fusion | flops 18874368 | bytes 31768576 | tf_op jit(solution)/shard_map/convert_element_type | solution.py:547
  317.2 2.3 fusion.40
  319.8 2.1 fusion.38
  325.8 4.1 convolution_convert_fusion.4
  329.9 223.3 %shard_map.204 = (f32[2,96,2304]{2,1,0:T(8,128)}, f32[2,96,768]{2,1,0:T(8,128)}, f32[2,96,3072]{2,1,0:T(8,128)}, f32[2,384,768]{2,1,0:T(8,128)}, f32[24,128]{1,0:T(8,128)}) custom-call(bf16[4,2,2,48,2304]{4,3,2,1,0:T(8,128)(2,1)} %bitcast.311, bf16[4,2,2,48,768]{4,3,2,1,0:T(8,128)(2,1)} %bitcast.302, bf16[4,2,2,48,3072]{4,3,2,1,0:T(8,128)(2,1)} %bitcast.294, ...), custom_call_target="tpu_custom_call" | custom-call | tf_op jit(solution)/shard_map/pallas_call | solution.py:472
  555.9 2.8 copy.129
  (381 shorter events, 77.6 us)
Async XLA Ops:
  3.3 133.6 %copy-start.80 = (f32[197]{0:T(256)}, f32[197]{0:T(256)S(1)}, u32[]{:S(2)}) copy-start(f32[197]{0:T(256)S(1)} %broadcast_multiply_fusion.3) | copy-start | bytes 2368
  5.1 131.9 %copy-start.78 = (f32[197]{0:T(256)}, f32[197]{0:T(256)S(1)}, u32[]{:S(2)}) copy-start(f32[197]{0:T(256)S(1)} %fusion.97) | copy-start | bytes 2368
  8.6 126.3 %copy-start.85 = (f32[512]{0:T(512)}, f32[512]{0:T(512)S(1)}, u32[]{:S(2)}) copy-start(f32[512]{0:T(512)S(1)} %fusion.39) | copy-start | bytes 6148
  11.3 125.6 %copy-start.6 = (bf16[1,197,768]{2,1,0:T(8,128)(2,1)S(1)}, bf16[1,197,768]{2,1,0:T(8,128)(2,1)}, u32[]{:S(2)}) copy-start(bf16[1,197,768]{2,1,0:T(8,128)(2,1)} %param.12) | copy-start | bytes 907780
  143.0 5.0 copy-start.111
  159.5 8.3 %copy-start.40 = (bf16[1,197,768]{2,1,0:T(8,128)(2,1)S(1)}, bf16[1,197,768]{2,1,0:T(8,128)(2,1)}, u32[]{:S(2)}) copy-start(bf16[1,197,768]{2,1,0:T(8,128)(2,1)} %param.13) | copy-start | bytes 907780
  167.8 5.5 copy-start.26
  167.8 5.5 copy-start.110
  173.3 4.8 copy-start.57
  173.3 4.8 copy-start.83
  173.3 4.8 copy-start.93
  189.3 4.9 copy-start.19
  214.0 5.3 copy-start.27
  225.0 4.6 copy-start
  225.0 4.6 copy-start.28
  232.8 21.5 %slice-start.5 = ((s8[4718592]{0:T(1024)(128)(4,1)}), s8[4194304]{0:T(1024)(128)(4,1)S(1)}, s32[]{:S(2)}) async-start(s8[4718592]{0:T(1024)(128)(4,1)} %bitcast.351), calls=%async_computation.5 | async-start | bytes 8388608
  232.9 33.3 %slice-start.3 = ((s8[4718592]{0:T(1024)(128)(4,1)}), s8[4194304]{0:T(1024)(128)(4,1)S(1)}, s32[]{:S(2)}) async-start(s8[4718592]{0:T(1024)(128)(4,1)} %bitcast.349), calls=%async_computation.3 | async-start | bytes 8388608
  233.8 32.3 %copy-start.13 = (f32[1,512,768]{2,1,0:T(8,128)}, f32[1,512,768]{2,1,0:T(8,128)S(1)}, u32[]{:S(2)}) copy-start(f32[1,512,768]{2,1,0:T(8,128)S(1)} %get-tuple-element.141) | copy-start | bytes 4718596
  234.2 20.2 %copy-start.32 = (bf16[1,512,768]{2,1,0:T(8,128)(2,1)S(1)}, bf16[1,512,768]{2,1,0:T(8,128)(2,1)}, u32[]{:S(2)}) copy-start(bf16[1,512,768]{2,1,0:T(8,128)(2,1)} %param.15) | copy-start | bytes 2359300
  234.2 20.2 %slice-start.6 = ((s8[4718592]{0:T(1024)(128)(4,1)}), s8[524288]{0:T(1024)(128)(4,1)S(1)}, s32[]{:S(2)}) async-start(s8[4718592]{0:T(1024)(128)(4,1)} %bitcast.351), calls=%async_computation.6 | async-start | bytes 1048576
  234.2 32.0 %slice-start.4 = ((s8[4718592]{0:T(1024)(128)(4,1)}), s8[524288]{0:T(1024)(128)(4,1)S(1)}, s32[]{:S(2)}) async-start(s8[4718592]{0:T(1024)(128)(4,1)} %bitcast.349), calls=%async_computation.4 | async-start | bytes 1048576
  254.3 8.3 %copy-start.118 = (bf16[512,3072]{1,0:T(8,128)(2,1)}, bf16[512,3072]{1,0:T(8,128)(2,1)S(1)}, u32[]{:S(2)}) copy-start(bf16[512,3072]{1,0:T(8,128)(2,1)S(1)} %get-tuple-element.115) | copy-start | bytes 9437188
  254.3 8.3 %copy-start.108 = (f32[768]{0:T(1024)S(1)}, f32[768]{0:T(1024)}, u32[]{:S(2)}) copy-start(f32[768]{0:T(1024)} %get-tuple-element.91) | copy-start | bytes 9220
  282.7 10.8 %copy-start.30 = (bf16[512,768]{0,1:T(8,128)(2,1)}, bf16[512,768]{0,1:T(8,128)(2,1)S(1)}, u32[]{:S(2)}) copy-start(bf16[512,768]{0,1:T(8,128)(2,1)S(1)} %copy.103) | copy-start | bytes 2359300
  286.2 7.3 %copy-start.33 = (bf16[1,512,768]{2,1,0:T(8,128)(2,1)S(1)}, bf16[1,512,768]{2,1,0:T(8,128)(2,1)}, u32[]{:S(2)}) copy-start(bf16[1,512,768]{2,1,0:T(8,128)(2,1)} %param.15) | copy-start | bytes 2359300
  286.2 7.3 %copy-start.119 = (bf16[512,3072]{1,0:T(8,128)(2,1)S(1)}, bf16[512,3072]{1,0:T(8,128)(2,1)}, u32[]{:S(2)}) copy-start(bf16[512,3072]{1,0:T(8,128)(2,1)} %copy-done.118) | copy-start | bytes 9437188
  286.2 11.7 %slice-start = ((s8[12582912]{0:T(1024)(128)(4,1)}), s8[4194304]{0:T(1024)(128)(4,1)S(1)}, s32[]{:S(2)}) async-start(s8[12582912]{0:T(1024)(128)(4,1)} %bitcast.291), calls=%async_computation | async-start | bytes 8388608
  286.2 11.7 %slice-start.1 = ((s8[12582912]{0:T(1024)(128)(4,1)}), s8[4194304]{0:T(1024)(128)(4,1)S(1)}, s32[]{:S(2)}) async-start(s8[12582912]{0:T(1024)(128)(4,1)} %bitcast.291), calls=%async_computation.1 | async-start | bytes 8388608
  293.5 4.4 slice-start.2
  304.9 7.2 %copy-start.8 = (bf16[1,512,768]{1,2,0:T(8,128)(2,1)S(1)}, bf16[1,512,768]{1,2,0:T(8,128)(2,1)}, u32[]{:S(2)}) copy-start(bf16[1,512,768]{1,2,0:T(8,128)(2,1)} %copy.96) | copy-start | bytes 2359300
  553.2 5.6 copy-start.63
  553.2 6.4 %copy-start.43 = (f32[2,96,3072]{2,1,0:T(8,128)S(1)}, f32[2,96,3072]{2,1,0:T(8,128)}, u32[]{:S(2)}) copy-start(f32[2,96,3072]{2,1,0:T(8,128)} %get-tuple-element.176) | copy-start | bytes 7077892
  (95 other events, 226.5 us)

commit v2 on v1

--- a/solution.py
+++ b/solution.py
@@ -8,6 +8,384 @@
 from jax.sharding import PartitionSpec as P
 
 HEAD = 64
+
+NT = (((1,), (1,)), ((), ()))
+TN = (((0,), (0,)), ((), ()))
+TILE = 256
+CHUNK = 64
+
+
+def dot(a, b, dims=(((1,), (0,)), ((), ()))):
+    return lax.dot_general(a, b, dims, preferred_element_type=jnp.float32)
+
+
+def at(t, size=TILE):
+    return pl.ds(pl.multiple_of(t * size, size), size)
+
+
+def layer_scratch(n, width, deep):
+    low, full = jnp.bfloat16, jnp.float32
+    return dict(
+        x=pltpu.VMEM((n, width), low),
+        dy=pltpu.VMEM((n, width), low),
+        a=pltpu.VMEM((n, width), low),
+        a_t=pltpu.VMEM((width, n), low),
+        qkv=pltpu.VMEM((n, 3 * width), low),
+        bias=pltpu.VMEM((n, n), full),
+        wt=pltpu.VMEM((width // HEAD, n, n), low),
+        ds=pltpu.VMEM((2, n, n), low),
+        o=pltpu.VMEM((n, width), low),
+        o_t=pltpu.VMEM((width, n), low),
+        h=pltpu.VMEM((n, width), full),
+        c=pltpu.VMEM((n, width), low),
+        c_t=pltpu.VMEM((width, n), low),
+        g=pltpu.VMEM((n, deep), low),
+        du=pltpu.VMEM((n, deep), low),
+        sums=pltpu.VMEM((n, width), full),
+        dh=pltpu.VMEM((n, width), full),
+        rows=pltpu.VMEM((8, 3 * width), full),
+        tall=pltpu.VMEM((2, width, TILE), low),
+        wide=pltpu.VMEM((2, TILE, width), low),
+        tall_sem=pltpu.SemaphoreType.DMA((2,)),
+        wide_sem=pltpu.SemaphoreType.DMA((2,)),
+    )
+
+
+class Layer:
+    def __init__(self, n, kept, weights, small, terms, outs):
+        self.n, self.s = n, kept
+        self.w_qkv, self.w_out, self.w_up, self.w_down = weights
+        self.par, self.b_up = small
+        self.g_qkv, self.g_out, self.g_up, self.g_down = terms
+        self.y_out, self.x_grad, self.g_par, self.g_bup = outs
+        self.width, self.deep = self.w_qkv.shape[0], self.w_up.shape[1]
+
+    def chunks(self, body):
+        def step(i, carry):
+            body(at(i, CHUNK))
+            return carry
+
+        lax.fori_loop(0, self.n // CHUNK, step, 0)
+
+    def tiles(self, first, last, body):
+        def step(i, carry):
+            body(i)
+            return carry
+
+        lax.fori_loop(first, last, step, 0)
+
+    def row(self, ref, i):
+        return ref[i : i + 1, :]
+
+    def tall_copy(self, ref, slot, t):
+        return pltpu.make_async_copy(self.s["tall"].at[slot], ref.at[:, at(t)], self.s["tall_sem"].at[slot])
+
+    def wide_copy(self, ref, slot, t):
+        return pltpu.make_async_copy(self.s["wide"].at[slot], ref.at[at(t)], self.s["wide_sem"].at[slot])
+
+    def put(self, copy, buf, ref, t, count, value):
+        slot = lax.rem(t, 2)
+        pl.when(t >= 2)(lambda: copy(ref, slot, t - 2).wait())
+        buf[slot] = value.astype(jnp.bfloat16)
+        copy(ref, slot, t).start()
+
+    def put_end(self, copy, ref, count):
+        for t in range(max(0, count - 2), count):
+            copy(ref, t % 2, t).wait()
+
+    def load(self, x, dy, seg_col, seg_row):
+        s, have = self.s, x.shape[0]
+        if have < self.n:
+            start = have // 16 * 16
+            s["x"][start:, :] = jnp.zeros((self.n - start, self.width), jnp.bfloat16)
+            s["dy"][start:, :] = jnp.zeros((self.n - start, self.width), jnp.bfloat16)
+        s["x"][0:have, :] = x[...]
+        s["dy"][0:have, :] = dy[...]
+        s["bias"][...] = jnp.where(seg_col[...] == seg_row[...], 0.0, -1e30)
+        self.g_par[...] = jnp.zeros_like(self.g_par)
+        width = self.width
+        s["rows"][0:1, 0:width] = self.par[4:5, :]
+        s["rows"][0:1, width : 2 * width] = jnp.zeros((1, width), jnp.float32)
+        s["rows"][0:1, 2 * width :] = self.par[5:6, :]
+
+    def norm_parts(self, values):
+        center = values - jnp.mean(values, axis=-1, keepdims=True)
+        scale = lax.rsqrt(jnp.mean(center * center, axis=-1, keepdims=True) + 1e-05)
+        return center * scale, scale
+
+    def norm(self, src, dst, which):
+        def body(rows):
+            unit, _ = self.norm_parts(src[rows, :].astype(jnp.float32))
+            dst[rows, :] = (unit * self.row(self.par, which) + self.row(self.par, 2 + which)).astype(jnp.bfloat16)
+
+        self.chunks(body)
+
+    def norm_a(self):
+        self.norm(self.s["x"], self.s["a"], 0)
+
+    def project(self):
+        s = self.s
+        queries = self.width // TILE
+
+        def body(t):
+            scale = jnp.where(t < queries, HEAD ** (-0.5), 1.0)
+            found = dot(s["a"][...], self.w_qkv[:, at(t)]) + s["rows"][0:1, at(t)]
+            s["qkv"][:, at(t)] = (found * scale).astype(jnp.bfloat16)
+
+        self.tiles(0, 3 * queries, body)
+        s["a_t"][...] = s["a"][...].T
+
+    def pair(self, i, which):
+        start = which * self.width + i * 128
+        return self.s["qkv"].at[:, pl.ds(pl.multiple_of(start, 128), 128)]
+
+    def own_lanes(self, value, head):
+        lanes = lax.broadcasted_iota(jnp.int32, value.shape, 1)
+        return jnp.where((lanes < HEAD) == (head == 0), value, jnp.zeros_like(value))
+
+    def attend(self, first, last):
+        s = self.s
+
+        def body(i):
+            q, k, v = (self.pair(i, which) for which in range(3))
+            keys = [self.own_lanes(k[...], head) for head in range(2)]
+            vals = [self.own_lanes(v[...], head) for head in range(2)]
+            for part in range(self.n // TILE):
+                cols = slice(part * TILE, part * TILE + TILE)
+                mixed = None
+                for head in range(2):
+                    scores = dot(keys[head], q[cols, :], NT) + s["bias"][:, cols]
+                    raised = jnp.exp(scores - jnp.max(scores, axis=0, keepdims=True))
+                    share = 1.0 / jnp.sum(raised, axis=0, keepdims=True)
+                    weights = (raised * share).astype(jnp.bfloat16)
+                    s["wt"][2 * i + head, :, cols] = weights
+                    found = dot(vals[head], weights, TN)
+                    mixed = found if mixed is None else mixed + found
+                s["o"][cols, at(i, 128)] = mixed.T.astype(jnp.bfloat16)
+
+        self.tiles(first, last, body)
+
+    def branch(self):
+        s = self.s
+
+        def body(t):
+            found = dot(s["o"][...], self.w_out[:, at(t)]) + self.par[6:7, at(t)]
+            s["h"][:, at(t)] = s["x"][:, at(t)].astype(jnp.float32) + found
+
+        self.tiles(0, self.width // TILE, body)
+        s["o_t"][...] = s["o"][...].T
+
+    def norm_c(self):
+        self.norm(self.s["h"], self.s["c"], 1)
+
+    def up(self, first, last):
+        s = self.s
+
+        def body(t):
+            before = dot(s["c"][...], self.w_up[:, at(t)]) + self.b_up[0:1, at(t)]
+            chance = 0.5 + 0.5 * lax.erf(before * 0.7071067811865476)
+            s["g"][:, at(t)] = (before * chance).astype(jnp.bfloat16)
+            slope = chance + before * (jnp.exp(before * before * -0.5) * 0.3989422804014327)
+            s["du"][:, at(t)] = slope.astype(jnp.bfloat16)
+
+        self.tiles(first, last, body)
+
+    def turn_c(self):
+        self.s["c_t"][...] = self.s["c"][...].T
+
+    def down(self):
+        s = self.s
+
+        def body(t):
+            found = dot(s["g"][...], self.w_down[:, at(t)]) + self.par[7:8, at(t)]
+            s["sums"][:, at(t)] = s["h"][:, at(t)] + found
+
+        self.tiles(0, self.width // TILE, body)
+        have = self.y_out.shape[0]
+        self.y_out[...] = s["sums"][0:have, :].astype(jnp.bfloat16)
+
+    def feed_back(self, first, last):
+        s = self.s
+        count = self.deep // TILE
+
+        def body(t):
+            grad = dot(s["dy"][...], self.w_down[at(t), :], NT)
+            low = (grad * s["du"][:, at(t)].astype(jnp.float32)).astype(jnp.bfloat16)
+            s["du"][:, at(t)] = low
+            self.g_bup[0:1, at(t)] = jnp.sum(low.astype(jnp.float32), axis=0, keepdims=True)
+            self.put(self.wide_copy, s["wide"], self.g_down, t, count, dot(s["g"][:, at(t)], s["dy"][...], TN))
+            self.put(self.tall_copy, s["tall"], self.g_up, t, count, dot(s["c_t"][...], low))
+
+        self.tiles(first, last, body)
+
+    def feed_end(self):
+        self.put_end(self.wide_copy, self.g_down, self.deep // TILE)
+        self.put_end(self.tall_copy, self.g_up, self.deep // TILE)
+
+    def up_back(self):
+        s = self.s
+
+        def body(t):
+            s["sums"][:, at(t)] = dot(s["du"][...], self.w_up[at(t), :], NT)
+
+        self.tiles(0, self.width // TILE, body)
+
+    def norm_back(self, src, which, grad, rest, body_out):
+        def body(rows):
+            unit, scale = self.norm_parts(src[rows, :].astype(jnp.float32))
+            came = grad[rows, :]
+            gained = came * self.row(self.par, which)
+            self.g_par[which : which + 1, :] += jnp.sum(came * unit, axis=0, keepdims=True)
+            self.g_par[2 + which : 3 + which, :] += jnp.sum(came, axis=0, keepdims=True)
+            inner = gained - jnp.mean(gained, axis=-1, keepdims=True)
+            inner = inner - unit * jnp.mean(gained * unit, axis=-1, keepdims=True)
+            body_out(rows, rest[rows, :].astype(jnp.float32) + inner * scale)
+
+        self.chunks(body)
+
+    def norm_c_back(self):
+        s = self.s
+
+        def keep(rows, grad):
+            s["dh"][rows, :] = grad
+            low = grad.astype(jnp.bfloat16)
+            s["c"][rows, :] = low
+            self.g_par[6:7, :] += jnp.sum(low.astype(jnp.float32), axis=0, keepdims=True)
+            self.g_par[7:8, :] += jnp.sum(s["dy"][rows, :].astype(jnp.float32), axis=0, keepdims=True)
+
+        self.norm_back(s["h"], 1, s["sums"], s["dy"], keep)
+
+    def branch_back(self):
+        s = self.s
+        count = self.width // TILE
+
+        def body(t):
+            s["a"][:, at(t)] = dot(s["c"][...], self.w_out[at(t), :], NT).astype(jnp.bfloat16)
+            self.put(self.tall_copy, s["tall"], self.g_out, t, count, dot(s["o_t"][...], s["c"][:, at(t)]))
+
+        self.tiles(0, count, body)
+        self.put_end(self.tall_copy, self.g_out, count)
+
+    def attend_back(self, first, last):
+        s, width = self.s, self.width
+
+        def body(i):
+            q, k, v = (self.pair(i, which) for which in range(3))
+            came = s["a"].at[:, at(i, 128)]
+            dq = dk = dv = None
+            for head in range(2):
+                vals = self.own_lanes(v[...], head)
+                for part in range(self.n // TILE):
+                    cols = slice(part * TILE, part * TILE + TILE)
+                    grad = dot(vals, came[cols, :], NT)
+                    weights = s["wt"][2 * i + head, :, cols].astype(jnp.float32)
+                    product = weights * grad
+                    inner = jnp.sum(product, axis=0, keepdims=True)
+                    s["ds"][head, :, cols] = (product - weights * inner).astype(jnp.bfloat16)
+                one_q = dot(self.own_lanes(k[...], head), s["ds"][head], TN)
+                one_k = dot(s["ds"][head], self.own_lanes(q[...], head))
+                one_v = dot(s["wt"][2 * i + head], self.own_lanes(came[...], head))
+                dq, dk, dv = (one_q, one_k, one_v) if head == 0 else (dq + one_q, dk + one_k, dv + one_v)
+            s["g"][:, at(i, 128)] = dq.T.astype(jnp.bfloat16) * HEAD ** (-0.5)
+            s["g"][:, pl.ds(pl.multiple_of(width + i * 128, 128), 128)] = dk.astype(jnp.bfloat16)
+            s["g"][:, pl.ds(pl.multiple_of(2 * width + i * 128, 128), 128)] = dv.astype(jnp.bfloat16)
+
+        self.tiles(first, last, body)
+
+    def project_terms(self):
+        s = self.s
+        count = 3 * self.width // TILE
+
+        def body(t):
+            grad = s["g"][:, at(t)]
+            s["rows"][1:2, at(t)] = jnp.sum(grad.astype(jnp.float32), axis=0, keepdims=True)
+            self.put(self.tall_copy, s["tall"], self.g_qkv, t, count, dot(s["a_t"][...], grad))
+
+        self.tiles(0, count, body)
+        self.put_end(self.tall_copy, self.g_qkv, count)
+        self.g_par[4:5, :] = s["rows"][1:2, 0 : self.width]
+        self.g_par[5:6, :] = s["rows"][1:2, 2 * self.width :]
+
+    def project_back(self):
+        s = self.s
+
+        def body(t):
+            s["sums"][:, at(t)] = dot(s["g"][:, 0 : 3 * self.width], self.w_qkv[at(t), :], NT)
+
+        self.tiles(0, self.width // TILE, body)
+
+    def norm_a_back(self):
+        s = self.s
+        have = self.x_grad.shape[0]
+
+        def keep(rows, grad):
+            s["dh"][rows, :] = grad
+
+        self.norm_back(s["x"], 0, s["sums"], s["dh"], keep)
+        self.x_grad[...] = s["dh"][0:have, :]
+
+
+def layer_kernel(n, names, *refs):
+    x, dy, seg_col, seg_row, par, b_up, *weights = refs[:10]
+    y_out, x_grad, g_par, g_bup, *terms = refs[10:18]
+    near, *held = refs[18:23]
+    kept = dict(zip(names, refs[23:]))
+    loads = [pltpu.make_async_copy(weights[i], held[i], near.at[i]) for i in range(4)]
+    for load in loads:
+        load.start()
+    layer = Layer(n, kept, held, (par, b_up), terms, (y_out.at[0], x_grad.at[0], g_par, g_bup))
+    heads, tiles = layer.width // 128, layer.deep // TILE
+    layer.load(x.at[0], dy.at[0], seg_col, seg_row)
+    layer.norm_a()
+    loads[0].wait()
+    layer.project()
+    layer.attend(0, heads)
+    loads[1].wait()
+    layer.branch()
+    layer.norm_c()
+    loads[2].wait()
+    layer.up(0, tiles)
+    layer.turn_c()
+    loads[3].wait()
+    layer.down()
+    layer.feed_back(0, tiles)
+    layer.feed_end()
+    layer.up_back()
+    layer.norm_c_back()
+    layer.branch_back()
+    layer.attend_back(0, heads)
+    layer.project_terms()
+    layer.project_back()
+    layer.norm_a_back()
+
+
+def padded(rows):
+    return -(-rows // TILE) * TILE
+
+
+def run_layer(x, dy, segment, weights, par, b_up):
+    have, width = x.shape[1:]
+    n, deep = padded(have), b_up.shape[1]
+    segment = jnp.pad(segment, ((0, 0), (0, n - have)), constant_values=-1)
+    kept = layer_scratch(n, width, deep)
+    anywhere, inside = pl.BlockSpec(memory_space=pl.ANY), pl.BlockSpec(memory_space=pltpu.VMEM)
+    outs = [
+        jax.ShapeDtypeStruct(x.shape, jnp.bfloat16),
+        jax.ShapeDtypeStruct(x.shape, jnp.float32),
+        jax.ShapeDtypeStruct(par.shape, jnp.float32),
+        jax.ShapeDtypeStruct(b_up.shape, jnp.float32),
+    ] + [jax.ShapeDtypeStruct(weight.shape, jnp.bfloat16) for weight in weights]
+    return pl.pallas_call(
+        functools.partial(layer_kernel, n, list(kept)),
+        out_shape=outs,
+        in_specs=[inside] * 6 + [anywhere] * 4,
+        out_specs=[inside] * 4 + [anywhere] * 4,
+        scratch_shapes=[pltpu.SemaphoreType.DMA((4,))]
+        + [pltpu.VMEM(weight.shape, weight.dtype) for weight in weights]
+        + list(kept.values()),
+        compiler_params=pltpu.CompilerParams(vmem_limit_bytes=62 * 2**20),
+    )(x, dy, segment.reshape(n, 1), segment, par, b_up, *weights)
+
 
 MESH = pl.DeviceIdType.MESH
 UP, DOWN, YWAY, XWAY, CORE, COREY, COREX = range(7)
@@ -835,13 +1213,14 @@
     outs, grads, terms, smalls = [], [], [], []
     image_seg = jnp.zeros((images.shape[0], images.shape[1]), jnp.int32)
     caption_seg = segment_ids(lengths, captions.shape[1])
+    par = jnp.concatenate([gains_all, biases_all], axis=1)
     for layer, (rows, cot, seg) in enumerate(((images, image_cot, image_seg), (captions, caption_cot, caption_seg))):
-        weights = (*fulls[layer * 4 : layer * 4 + 4], gains_all[layer], biases_all[layer], up_all[layer])
-        result, grad, found = backward_layer(rows, cot, weights, seg)
+        weights = fulls[layer * 4 : layer * 4 + 4]
+        result, grad, g_par, g_bup, *found = run_layer(rows, cot, seg, weights, par[layer], up_all[layer : layer + 1])
         outs.append(result)
         grads.append(grad)
-        terms += [term.astype(jnp.bfloat16) for term in found[:4]]
-        smalls.append(found[4:])
+        terms += found
+        smalls.append((g_par[:2], g_par[2:], g_bup[0]))
     packed = spread_small(count, *(jnp.stack([smalls[0][at], smalls[1][at]]) for at in range(3)))
     *shares, small_share = reduce_all(line, terms, packed)
     rest = unpack_small(small_share[None], width, deep)

time: 569 us -> 485 us (0.85)
  matrix products: 130 us -> 0 us
  Pallas kernels: 345 us -> 460 us
  other arithmetic: 38 us -> 1.63 us
  local copies, waits for them, and re-layouts: 48.2 us -> 21.7 us
    dot_general x36 -> x0, matrix products: 130 us -> none  [the longest x2 28.4 us: forward_layer(): jnp.einsum('bld,df->blf', normed_c, up_weight, preferred_element_type=jnp...]
    pallas_call x0 -> x2, Pallas kernels: none -> 115 us  [run_layer(): pl.pallas_call(functools.partial(layer_kernel, n, list(kept)), out_shape=...]
    reduce_sum x22 -> x0, other arithmetic: 22.4 us -> none  [the longest x4 6.56 us: normed(): center = values - jnp.mean(values, axis=-1, keepdims=True)]
    unnamed x264 -> x32, local copies, waits for them, and re-layouts: 23.8 us -> 13.3 us
    convert_element_type x4 -> x0, other arithmetic: 9.25 us -> none  [the longest x2 7.73 us: attention_back(): grad_scores = (attn_weights * (grad_weights - inner)).astype(jnp.bfloat16)]
    convert_element_type x6 -> x0, local copies, waits for them, and re-layouts: 8.98 us -> none  [the longest x2 3.29 us: backward_layer(): grad_mixed = jnp.einsum('ble,de->bld', grad_branch, out_weight, preferred...]
where the time goes in v2:
time: 485 us; the launch traced here: 484 us
  Pallas kernels  460 us (95%)
  local copies, waits for them, and re-layouts  21.7 us (4%)
    pallas_call x1, Pallas kernels, reduce_all(): pl.pallas_call(functools.partial(reduce_kernel, line, order), out_shape=o...  223 us
    pallas_call x1, Pallas kernels, gather_all(): pl.pallas_call(functools.partial(gather_kernel, line, order), out_shape=o...  122 us
    pallas_call x2, Pallas kernels, run_layer(): pl.pallas_call(functools.partial(layer_kernel, n, list(kept)), out_shape=...  115 us
    unnamed x32, local copies, waits for them, and re-layouts  13.3 us

profile of v2, /device:TPU:9, one launch (start us, length us, event | category | flops | bytes accessed | tf_op | source)
XLA Modules:
  0.0 484.0 jit_solution(15737385240467919071)
XLA Ops:
  0.7 0.7 copy.33
  1.4 0.8 reshape.153
  2.2 0.8 concatenate.10
  3.0 0.6 bitcast_convert_fusion.refs_4_
  3.6 121.6 %shard_map.203 = (bf16[768,2304]{1,0:T(8,128)(2,1)}, bf16[768,768]{1,0:T(8,128)(2,1)}, bf16[768,3072]{1,0:T(8,128)(2,1)}, bf16[3072,768]{1,0:T(8,128)(2,1)}, bf1...) custom-call(bf16[2,96,2304]{2,1,0:T(8,128)(2,1)} %refs_0_.3, ...), custom_call_target="tpu_custom_call" | custom-call | tf_op jit(solution)/shard_map/pallas_call | solution.py:625
  125.2 0.9 copy.52
  126.2 0.1 reshape.159
  126.3 0.7 squeeze.7.refs_4_
  127.0 0.6 copy.43
  127.6 0.2 reduce_window_sum.11
  127.9 0.9 copy.36.refs_2_
  128.8 70.1 %shard_map.205 = (bf16[1,512,768]{2,1,0:T(8,128)(2,1)}, f32[1,512,768]{2,1,0:T(8,128)}, f32[8,768]{1,0:T(8,128)}, f32[1,3072]{1,0:T(1,128)}, bf16[768,2304]{1,0:...) custom-call(bf16[1,512,768]{2,1,0:T(8,128)(2,1)} %refs_0_.5, ...), custom_call_target="tpu_custom_call" | custom-call | tf_op jit(solution)/shard_map/pallas_call | solution.py:378
  198.9 0.7 squeeze.6.refs_4_
  199.6 0.6 copy.42
  200.2 0.8 copy.35.refs_2_
  201.0 44.7 %shard_map.204 = (bf16[1,197,768]{2,1,0:T(8,128)(2,1)}, f32[1,197,768]{2,1,0:T(8,128)}, f32[8,768]{1,0:T(8,128)}, f32[1,3072]{1,0:T(1,128)}, bf16[768,2304]{1,0:...) custom-call(bf16[1,197,768]{2,1,0:T(8,128)(2,1)} %refs_0_.4, ...), custom_call_target="tpu_custom_call" | custom-call | tf_op jit(solution)/shard_map/pallas_call | solution.py:378
  245.7 0.7 slice_bitcast_fusion.5
  246.5 0.7 slice_bitcast_fusion.1
  247.2 0.1 reshape.169
  247.4 0.7 pad_maximum_fusion.1
  248.2 0.7 copy.51
  248.9 223.3 %shard_map.206 = (f32[2,96,2304]{2,1,0:T(8,128)}, f32[2,96,768]{2,1,0:T(8,128)}, f32[2,96,3072]{2,1,0:T(8,128)}, f32[2,384,768]{2,1,0:T(8,128)}, f32[24,128]{1,0:T(8,128)}) custom-call(bf16[4,2,2,48,2304]{4,3,2,1,0:T(8,128)(2,1)} %bitcast.74, bf16[4,2,2,48,768]{4,3,2,1,0:T(8,128)(2,1)} %bitcast.76, bf16[4,2,2,48,3072]{4,3,2,1,0:T(8,128)(2,1)} %bitcast.71, ...), custom_call_target="tpu_custom_call" | custom-call | tf_op jit(solution)/shard_map/pallas_call | solution.py:850
  472.2 0.7 slice_reduce_fusion
  473.1 0.6 copy.40
  473.7 0.6 slice.87
  474.2 0.6 slice_bitcast_fusion.7
  474.8 1.4 copy.39
  476.3 2.9 copy.60
  479.2 0.8 copy.61
  480.0 1.4 copy.62
  481.4 1.1 copy-done
  482.6 1.4 copy.63
  (38 shorter events, 0.5 us)
Async XLA Ops:
  0.6 127.0 %copy-start.8 = (s32[1,8]{1,0:T(1,128)S(1)}, s32[1,8]{1,0:T(1,128)}, u32[]{:S(2)}) copy-start(s32[1,8]{1,0:T(1,128)} %param.16) | copy-start | bytes 100
  127.9 0.9 copy-start.5
  200.2 0.8 copy-start.7
  201.0 44.7 %copy-start.4 = (f32[8,768]{1,0:T(8,128)S(1)}, f32[8,768]{1,0:T(8,128)}, u32[]{:S(2)}) copy-start(f32[8,768]{1,0:T(8,128)} %get-tuple-element.63) | copy-start | bytes 73732
  201.0 46.4 %copy-start.6 = (f32[1,3072]{1,0:T(1,128)S(1)}, f32[1,3072]{1,0:T(1,128)}, u32[]{:S(2)}) copy-start(f32[1,3072]{1,0:T(1,128)} %get-tuple-element.65) | copy-start | bytes 36868
  248.9 225.9 %copy-start.2 = (f32[1,197,768]{2,1,0:T(8,128)S(1)}, f32[1,197,768]{2,1,0:T(8,128)}, u32[]{:S(2)}) copy-start(f32[1,197,768]{2,1,0:T(8,128)} %get-tuple-element.95) | copy-start | bytes 1815556
  474.8 4.4 copy-start.3
  476.3 3.8 copy-start.1
  480.0 2.5 copy-start

commit v3 on v2

--- a/solution.py
+++ b/solution.py
@@ -19,11 +19,15 @@
     return lax.dot_general(a, b, dims, preferred_element_type=jnp.float32)
 
 
+def flat(value):
+    return value.reshape(-1, value.shape[-1])
+
+
 def at(t, size=TILE):
     return pl.ds(pl.multiple_of(t * size, size), size)
 
 
-def layer_scratch(n, width, deep):
+def layer_scratch(n, width, deep, split):
     low, full = jnp.bfloat16, jnp.float32
     return dict(
         x=pltpu.VMEM((n, width), low),
@@ -44,8 +48,8 @@
         sums=pltpu.VMEM((n, width), full),
         dh=pltpu.VMEM((n, width), full),
         rows=pltpu.VMEM((8, 3 * width), full),
-        tall=pltpu.VMEM((2, width, TILE), low),
-        wide=pltpu.VMEM((2, TILE, width), low),
+        tall=pltpu.VMEM((2, *split, width), low),
+        wide=pltpu.VMEM((2, *split[1:3], deep // width, split[3], width), low),
         tall_sem=pltpu.SemaphoreType.DMA((2,)),
         wide_sem=pltpu.SemaphoreType.DMA((2,)),
     )
@@ -58,7 +62,7 @@
         self.par, self.b_up = small
         self.g_qkv, self.g_out, self.g_up, self.g_down = terms
         self.y_out, self.x_grad, self.g_par, self.g_bup = outs
-        self.width, self.deep = self.w_qkv.shape[0], self.w_up.shape[1]
+        self.width, self.deep = self.w_out.shape[-1], self.w_up.shape[-1]
 
     def chunks(self, body):
         def step(i, carry):
@@ -78,15 +82,16 @@
         return ref[i : i + 1, :]
 
     def tall_copy(self, ref, slot, t):
-        return pltpu.make_async_copy(self.s["tall"].at[slot], ref.at[:, at(t)], self.s["tall_sem"].at[slot])
+        cols = at(t, self.width)
+        return pltpu.make_async_copy(self.s["tall"].at[slot], ref.at[:, :, :, :, cols], self.s["tall_sem"].at[slot])
 
     def wide_copy(self, ref, slot, t):
-        return pltpu.make_async_copy(self.s["wide"].at[slot], ref.at[at(t)], self.s["wide_sem"].at[slot])
+        return pltpu.make_async_copy(self.s["wide"].at[slot], ref.at[t], self.s["wide_sem"].at[slot])
 
     def put(self, copy, buf, ref, t, count, value):
-        slot = lax.rem(t, 2)
+        slot = t % 2
         pl.when(t >= 2)(lambda: copy(ref, slot, t - 2).wait())
-        buf[slot] = value.astype(jnp.bfloat16)
+        buf[slot] = value.astype(jnp.bfloat16).reshape(buf.shape[1:])
         copy(ref, slot, t).start()
 
     def put_end(self, copy, ref, count):
@@ -129,7 +134,7 @@
 
         def body(t):
             scale = jnp.where(t < queries, HEAD ** (-0.5), 1.0)
-            found = dot(s["a"][...], self.w_qkv[:, at(t)]) + s["rows"][0:1, at(t)]
+            found = dot(s["a"][...], flat(self.w_qkv[:, :, :, :, at(t)])) + s["rows"][0:1, at(t)]
             s["qkv"][:, at(t)] = (found * scale).astype(jnp.bfloat16)
 
         self.tiles(0, 3 * queries, body)
@@ -169,7 +174,7 @@
         s = self.s
 
         def body(t):
-            found = dot(s["o"][...], self.w_out[:, at(t)]) + self.par[6:7, at(t)]
+            found = dot(s["o"][...], flat(self.w_out[:, :, :, :, at(t)])) + self.par[6:7, at(t)]
             s["h"][:, at(t)] = s["x"][:, at(t)].astype(jnp.float32) + found
 
         self.tiles(0, self.width // TILE, body)
@@ -182,7 +187,7 @@
         s = self.s
 
         def body(t):
-            before = dot(s["c"][...], self.w_up[:, at(t)]) + self.b_up[0:1, at(t)]
+            before = dot(s["c"][...], flat(self.w_up[:, :, :, :, at(t)])) + self.b_up[0:1, at(t)]
             chance = 0.5 + 0.5 * lax.erf(before * 0.7071067811865476)
             s["g"][:, at(t)] = (before * chance).astype(jnp.bfloat16)
             slope = chance + before * (jnp.exp(before * before * -0.5) * 0.3989422804014327)
@@ -197,7 +202,7 @@
         s = self.s
 
         def body(t):
-            found = dot(s["g"][...], self.w_down[:, at(t)]) + self.par[7:8, at(t)]
+            found = dot(s["g"][...], flat(self.w_down[:, :, :, :, :, at(t)])) + self.par[7:8, at(t)]
             s["sums"][:, at(t)] = s["h"][:, at(t)] + found
 
         self.tiles(0, self.width // TILE, body)
@@ -206,29 +211,25 @@
 
     def feed_back(self, first, last):
         s = self.s
-        count = self.deep // TILE
+        count, width = self.deep // self.width, self.width
 
         def body(t):
-            grad = dot(s["dy"][...], self.w_down[at(t), :], NT)
-            low = (grad * s["du"][:, at(t)].astype(jnp.float32)).astype(jnp.bfloat16)
-            s["du"][:, at(t)] = low
-            self.g_bup[0:1, at(t)] = jnp.sum(low.astype(jnp.float32), axis=0, keepdims=True)
-            self.put(self.wide_copy, s["wide"], self.g_down, t, count, dot(s["g"][:, at(t)], s["dy"][...], TN))
+            cols = at(t, width)
+            grad = dot(s["dy"][...], flat(self.w_down[t]), NT)
+            low = (grad * s["du"][:, cols].astype(jnp.float32)).astype(jnp.bfloat16)
+            s["du"][:, cols] = low
+            self.g_bup[0:1, cols] = jnp.sum(low.astype(jnp.float32), axis=0, keepdims=True)
+            self.put(self.wide_copy, s["wide"], self.g_down, t, count, dot(s["g"][:, cols], s["dy"][...], TN))
             self.put(self.tall_copy, s["tall"], self.g_up, t, count, dot(s["c_t"][...], low))
 
         self.tiles(first, last, body)
 
     def feed_end(self):
-        self.put_end(self.wide_copy, self.g_down, self.deep // TILE)
-        self.put_end(self.tall_copy, self.g_up, self.deep // TILE)
+        self.put_end(self.wide_copy, self.g_down, self.deep // self.width)
+        self.put_end(self.tall_copy, self.g_up, self.deep // self.width)
 
     def up_back(self):
-        s = self.s
-
-        def body(t):
-            s["sums"][:, at(t)] = dot(s["du"][...], self.w_up[at(t), :], NT)
-
-        self.tiles(0, self.width // TILE, body)
+        self.s["sums"][...] = dot(self.s["du"][...], flat(self.w_up[...]), NT)
 
     def norm_back(self, src, which, grad, rest, body_out):
         def body(rows):
@@ -257,14 +258,9 @@
 
     def branch_back(self):
         s = self.s
-        count = self.width // TILE
-
-        def body(t):
-            s["a"][:, at(t)] = dot(s["c"][...], self.w_out[at(t), :], NT).astype(jnp.bfloat16)
-            self.put(self.tall_copy, s["tall"], self.g_out, t, count, dot(s["o_t"][...], s["c"][:, at(t)]))
-
-        self.tiles(0, count, body)
-        self.put_end(self.tall_copy, self.g_out, count)
+        self.put(self.tall_copy, s["tall"], self.g_out, 0, 1, dot(s["o_t"][...], s["c"][...]))
+        s["a"][...] = dot(s["c"][...], flat(self.w_out[...]), NT).astype(jnp.bfloat16)
+        self.put_end(self.tall_copy, self.g_out, 1)
 
     def attend_back(self, first, last):
         s, width = self.s, self.width
@@ -294,11 +290,11 @@
 
     def project_terms(self):
         s = self.s
-        count = 3 * self.width // TILE
+        count, width = 3, self.width
 
         def body(t):
-            grad = s["g"][:, at(t)]
-            s["rows"][1:2, at(t)] = jnp.sum(grad.astype(jnp.float32), axis=0, keepdims=True)
+            grad = s["g"][:, at(t, width)]
+            s["rows"][1:2, at(t, width)] = jnp.sum(grad.astype(jnp.float32), axis=0, keepdims=True)
             self.put(self.tall_copy, s["tall"], self.g_qkv, t, count, dot(s["a_t"][...], grad))
 
         self.tiles(0, count, body)
@@ -308,11 +304,7 @@
 
     def project_back(self):
         s = self.s
-
-        def body(t):
-            s["sums"][:, at(t)] = dot(s["g"][:, 0 : 3 * self.width], self.w_qkv[at(t), :], NT)
-
-        self.tiles(0, self.width // TILE, body)
+        s["sums"][...] = dot(s["g"][:, 0 : 3 * self.width], flat(self.w_qkv[...]), NT)
 
     def norm_a_back(self):
         s = self.s
@@ -334,7 +326,7 @@
     for load in loads:
         load.start()
     layer = Layer(n, kept, held, (par, b_up), terms, (y_out.at[0], x_grad.at[0], g_par, g_bup))
-    heads, tiles = layer.width // 128, layer.deep // TILE
+    heads, tiles, panels = layer.width // 128, layer.deep // TILE, layer.deep // layer.width
     layer.load(x.at[0], dy.at[0], seg_col, seg_row)
     layer.norm_a()
     loads[0].wait()
@@ -348,7 +340,7 @@
     layer.turn_c()
     loads[3].wait()
     layer.down()
-    layer.feed_back(0, tiles)
+    layer.feed_back(0, panels)
     layer.feed_end()
     layer.up_back()
     layer.norm_c_back()
@@ -367,7 +359,7 @@
     have, width = x.shape[1:]
     n, deep = padded(have), b_up.shape[1]
     segment = jnp.pad(segment, ((0, 0), (0, n - have)), constant_values=-1)
-    kept = layer_scratch(n, width, deep)
+    kept = layer_scratch(n, width, deep, weights[1].shape[:4])
     anywhere, inside = pl.BlockSpec(memory_space=pl.ANY), pl.BlockSpec(memory_space=pltpu.VMEM)
     outs = [
         jax.ShapeDtypeStruct(x.shape, jnp.bfloat16),
@@ -1208,19 +1200,61 @@
     count = mesh.shape["fsdp"]
     line = count // 2
     width, deep = gains.shape[2], b_up.shape[1]
-    *fulls, small = gather_all(line, (w_qkv, w_out, w_up, w_down), pack_small(gains, biases, b_up))
-    gains_all, biases_all, up_all = unpack_small(small, width, deep)
-    outs, grads, terms, smalls = [], [], [], []
     image_seg = jnp.zeros((images.shape[0], images.shape[1]), jnp.int32)
     caption_seg = segment_ids(lengths, captions.shape[1])
+    own = tuple(w.reshape(2, 2, -1, w.shape[2]) for w in (w_qkv, w_out, w_up)) + (w_down.reshape(2, 2, 4, -1, w_down.shape[2]),)
+    n = padded(images.shape[1])
+    kept = layer_scratch(n, 768, 3072, (line, 2, 2, 48))
+    order = [(layer, which) for layer in range(2) for which in range(4)]
+    anywhere, inside = pl.BlockSpec(memory_space=pl.ANY), pl.BlockSpec(memory_space=pltpu.VMEM)
+    wshape = [(line, 2, 2, 48, 2304), (line, 2, 2, 48, 768), (line, 2, 2, 48, 3072), (line, 2, 2, 4, 48, 768)]
+    flatshape = [(768, 2304), (768, 768), (768, 3072), (3072, 768)]
+    outs = [jax.ShapeDtypeStruct(flatshape[which], jnp.bfloat16) for layer in range(2) for which in range(4)]
+    packed_small = pack_small(gains, biases, b_up)
+    outs.append(jax.ShapeDtypeStruct((2 * line, *packed_small.shape), jnp.float32))
+    outs += [
+        jax.ShapeDtypeStruct(images.shape, jnp.bfloat16),
+        jax.ShapeDtypeStruct(images.shape, jnp.float32),
+        jax.ShapeDtypeStruct((8, 768), jnp.float32),
+        jax.ShapeDtypeStruct((1, 3072), jnp.float32),
+    ] + [jax.ShapeDtypeStruct(shape, jnp.bfloat16) for shape in wshape]
+    sems = [
+            pltpu.SemaphoreType.DMA((8, 7, line)),
+            pltpu.SemaphoreType.DMA((8, 7, line)),
+            pltpu.SemaphoreType.DMA((8,)),
+            pltpu.SemaphoreType.DMA((2 * line,)),
+            pltpu.SemaphoreType.DMA((2 * line,)),
+    ]
+    ln = [pltpu.SemaphoreType.DMA((4,))] + [pltpu.VMEM(shape, jnp.bfloat16) for shape in wshape]
+    def merged(*refs):
+        owned, small = refs[:4], refs[4]
+        x, dy, seg_col, seg_row, par, b_upr = refs[5:11]
+        fulls, small_all = refs[11:19], refs[19]
+        y_out, x_grad, g_par, g_bup, *terms = refs[20:28]
+        scr = refs[28:]
+        gather_kernel(line, order, *owned, small, *fulls, small_all, *scr[:5])
+        weights=[fulls[0].reshape(*wshape[0]),fulls[1].reshape(*wshape[1]),fulls[2].reshape(*wshape[2]),fulls[3].reshape(*wshape[3])]
+        layer_kernel(n, list(kept), x, dy, seg_col, seg_row, par, b_upr, *weights, y_out, x_grad, g_par, g_bup, *terms, *scr[5:])
+    segment = jnp.pad(image_seg, ((0, 0), (0, n - 197)), constant_values=-1)
+    gains_all, biases_all, up_all = (
+        lax.all_gather(part.astype(jnp.float32), "fsdp", axis=part.ndim - 1, tiled=True) for part in (gains, biases, b_up)
+    )
     par = jnp.concatenate([gains_all, biases_all], axis=1)
-    for layer, (rows, cot, seg) in enumerate(((images, image_cot, image_seg), (captions, caption_cot, caption_seg))):
-        weights = fulls[layer * 4 : layer * 4 + 4]
-        result, grad, g_par, g_bup, *found = run_layer(rows, cot, seg, weights, par[layer], up_all[layer : layer + 1])
-        outs.append(result)
-        grads.append(grad)
-        terms += found
-        smalls.append((g_par[:2], g_par[2:], g_bup[0]))
+    res = pl.pallas_call(merged, out_shape=outs, in_specs=[anywhere] * 5 + [inside] * 6,
+        out_specs=[anywhere] * 9 + [inside] * 4 + [anywhere] * 4,
+        scratch_shapes=sems + ln + list(kept.values()),
+        compiler_params=pltpu.CompilerParams(collective_id=0, has_side_effects=True, vmem_limit_bytes=62 * 2**20))(
+        w_qkv, w_out, w_up, w_down, packed_small, images, image_cot, segment.reshape(n, 1), segment, par[0], up_all[:1])
+    fulls, small = res[:8], res[8]
+    outs, grads, terms, smalls = [res[9]], [res[10]], [t.reshape(-1, t.shape[-1]) for t in res[13:]], [(res[11][:2], res[11][2:], res[12][0])]
+    rows, cot, seg, layer = captions, caption_cot, caption_seg, 1
+    weights = fulls[layer * 4 : layer * 4 + 4]
+    weights = [w.reshape(line, 2, 2, -1, w.shape[1]) for w in weights[:3]] + [weights[3].reshape(line, 2, 2, 4, -1, weights[3].shape[1])]
+    result, grad, g_par, g_bup, *found = run_layer(rows, cot, seg, weights, par[layer], up_all[layer : layer + 1])
+    outs.append(result)
+    grads.append(grad)
+    terms += [t.reshape(-1, t.shape[-1]) for t in found]
+    smalls.append((g_par[:2], g_par[2:], g_bup[0]))
     packed = spread_small(count, *(jnp.stack([smalls[0][at], smalls[1][at]]) for at in range(3)))
     *shares, small_share = reduce_all(line, terms, packed)
     rest = unpack_small(small_share[None], width, deep)

time: 485 us -> 573 us (1.18)
  blocking collectives: 0 us -> 73.9 us
  Pallas kernels: 460 us -> 471 us
    all_gather x0 -> x3, blocking collectives: none -> 73.9 us  [local(): lax.all_gather(part.astype(jnp.float32), 'fsdp', axis=part.ndim - 1, tile...]
    pallas_call x1, Pallas kernels: 122 us -> 177 us  [local(): pl.pallas_call(merged, out_shape=outs, in_specs=[anywhere] * 5 + [inside]...]
    pallas_call x2 -> x1, Pallas kernels: 115 us -> 68.1 us  [run_layer(): pl.pallas_call(functools.partial(layer_kernel, n, list(kept)), out_shape=...]
    unnamed x32 -> x27, local copies, waits for them, and re-layouts: 13.3 us -> 12.9 us
where the time goes in v3:
time: 573 us; the launch traced here: 572 us
  Pallas kernels  471 us (82%)
  blocking collectives  73.9 us (13%)
  local copies, waits for them, and re-layouts  22.9 us (4%)
    pallas_call x1, Pallas kernels, reduce_all(): pl.pallas_call(functools.partial(reduce_kernel, line, order), out_shape=o...  226 us
    pallas_call x1, Pallas kernels, local(): pl.pallas_call(merged, out_shape=outs, in_specs=[anywhere] * 5 + [inside]...  177 us
    all_gather x3, blocking collectives, local(): lax.all_gather(part.astype(jnp.float32), 'fsdp', axis=part.ndim - 1, tile...  73.9 us
    pallas_call x1, Pallas kernels, run_layer(): pl.pallas_call(functools.partial(layer_kernel, n, list(kept)), out_shape=...  68.1 us
    unnamed x27, local copies, waits for them, and re-layouts  12.9 us

profile of v3, /device:TPU:9, one launch (start us, length us, event | category | flops | bytes accessed | tf_op | source)
XLA Modules:
  0.0 572.3 jit_solution(15721882630471956463)
XLA Ops:
  0.6 0.8 reduce_window_sum.11
  1.5 0.8 reshape.123
  2.3 0.7 convert_element_type.32
  3.0 0.7 copy.53
  3.8 0.8 concatenate.12
  4.6 0.6 bitcast_convert_fusion.refs_4_
  5.2 21.6 %all_gather.11 = f32[2,3072]{1,0:T(2,128)S(1)} all-gather(f32[2,384]{1,0:T(2,128)S(1)} %convert_element_type.32), channel_id=1, replica_groups=mesh['dp'=4,'fsdp'=8] {'fsdp'}, dimensions={1}, use_global_device_ids=true | all-gather | bytes 27648 | tf_op jit(solution)/shard_map/all_gather | solution.py:1240
  26.8 0.6 fusion.3
  27.4 0.8 copy.54
  28.2 0.8 copy.55
  29.0 0.8 copy.58.refs_7_
  29.8 0.9 copy.59.refs_2_
  30.7 26.6 %all_gather.10 = f32[2,6,768]{1,0,2:T(2,128)S(1)} all-gather(f32[2,6,96]{1,0,2:T(2,128)S(1)} %copy.55), channel_id=1, replica_groups=mesh['dp'=4,'fsdp'=8] {'fsdp'}, dimensions={2}, use_global_device_ids=true | all-gather | bytes 41472 | tf_op jit(solution)/shard_map/all_gather | solution.py:1240
  57.7 25.7 %all_gather.9 = f32[2,2,768]{1,0,2:T(2,128)S(1)} all-gather(f32[2,2,96]{1,0,2:T(2,128)S(1)} %copy.54), channel_id=1, replica_groups=mesh['dp'=4,'fsdp'=8] {'fsdp'}, dimensions={2}, use_global_device_ids=true | all-gather | bytes 13824 | tf_op jit(solution)/shard_map/all_gather | solution.py:1240
  83.8 0.6 fusion.2
  84.4 177.3 %shard_map.203 = (bf16[768,2304]{1,0:T(8,128)(2,1)}, bf16[768,768]{1,0:T(8,128)(2,1)}, bf16[768,3072]{1,0:T(8,128)(2,1)}, bf16[3072,768]{1,0:T(8,128)(2,1)}, bf1...) custom-call(bf16[2,96,2304]{2,1,0:T(8,128)(2,1)} %refs_0_.2, ...), custom_call_target="tpu_custom_call" | custom-call | tf_op jit(solution)/shard_map/pallas_call | solution.py:1243
  261.7 2.5 copy.62
  264.3 68.1 %shard_map.204 = (bf16[1,512,768]{2,1,0:T(8,128)(2,1)}, f32[1,512,768]{2,1,0:T(8,128)}, f32[8,768]{1,0:T(8,128)}, f32[1,3072]{1,0:T(1,128)}, bf16[4,2,2,48,2304]...) custom-call(bf16[1,512,768]{2,1,0:T(8,128)(2,1)} %refs_0_.3, ...), custom_call_target="tpu_custom_call" | custom-call | tf_op jit(solution)/shard_map/pallas_call | solution.py:370
  332.4 0.7 pad_maximum_fusion.2
  333.2 0.7 slice_bitcast_fusion.2
  333.9 0.7 slice_bitcast_fusion
  334.9 0.7 copy.69
  335.6 225.7 %shard_map.205 = (f32[2,96,2304]{2,1,0:T(8,128)}, f32[2,96,768]{2,1,0:T(8,128)}, f32[2,96,3072]{2,1,0:T(8,128)}, f32[2,384,768]{2,1,0:T(8,128)}, f32[24,128]{1,0:T(8,128)}) custom-call(bf16[4,2,2,48,2304]{4,3,2,1,0:T(8,128)(2,1)} %get-tuple-element.44.refs_0_, bf16[4,2,2,48,768]{4,3,2,1,0:T(8,128)(2,1)} %get-tuple-element.45.refs_1_, ...), custom_call_target="tpu_custom_call" | custom-call | tf_op jit(solution)/shard_map/pallas_call | solution.py:842
  561.3 0.8 slice_reduce_fusion
  562.7 0.6 slice.58
  563.3 0.6 copy.63
  563.9 0.7 copy.77
  564.6 2.9 copy.78
  567.6 0.8 copy.79
  568.4 1.4 copy.80
  569.8 1.1 copy-done
  570.9 1.4 copy.81
  (34 shorter events, 1.9 us)
Async XLA Ops:
  2.2 82.2 %copy-start.7 = (s32[256]{0:T(256)}, s32[256]{0:T(256)S(1)}, u32[]{:S(2)}) copy-start(s32[256]{0:T(256)S(1)} %pad.16) | copy-start | bytes 3076
  2.3 259.4 %copy-start.5 = (s32[512]{0:T(512)}, s32[512]{0:T(512)S(1)}, u32[]{:S(2)}) copy-start(s32[512]{0:T(512)S(1)} %convert_reduce_fusion) | copy-start | bytes 6148
  264.3 68.1 %copy-start.6 = (f32[1,3072]{1,0:T(1,128)S(1)}, f32[1,3072]{1,0:T(1,128)}, u32[]{:S(2)}) copy-start(f32[1,3072]{1,0:T(1,128)} %get-tuple-element.54) | copy-start | bytes 36868
  264.3 68.9 %copy-start.4 = (f32[8,768]{1,0:T(8,128)S(1)}, f32[8,768]{1,0:T(8,128)}, u32[]{:S(2)}) copy-start(f32[8,768]{1,0:T(8,128)} %get-tuple-element.52) | copy-start | bytes 73732
  335.6 228.4 %copy-start.3 = (bf16[1,197,768]{2,1,0:T(8,128)(2,1)S(1)}, bf16[1,197,768]{2,1,0:T(8,128)(2,1)}, u32[]{:S(2)}) copy-start(bf16[1,197,768]{2,1,0:T(8,128)(2,1)} %get-tuple-element.135) | copy-start | bytes 907780
  561.3 6.3 %copy-start.2 = (f32[2,96,768]{2,1,0:T(8,128)S(1)}, f32[2,96,768]{2,1,0:T(8,128)}, u32[]{:S(2)}) copy-start(f32[2,96,768]{2,1,0:T(8,128)} %get-tuple-element.140) | copy-start | bytes 1769476
  564.6 3.8 copy-start.1
  568.4 2.5 copy-start

commit v4 on v0

--- a/solution.py
+++ b/solution.py
@@ -1,9 +1,1056 @@
+import functools
+
 import jax
 import jax.numpy as jnp
 from jax import lax
+from jax.experimental import pallas as pl
+from jax.experimental.pallas import tpu as pltpu
 from jax.sharding import PartitionSpec as P
 
 HEAD = 64
+
+MESH = pl.DeviceIdType.MESH
+NT = (((1,), (1,)), ((), ()))
+TN = (((0,), (0,)), ((), ()))
+TILE = 256
+CHUNK = 64
+ALL = slice(None)
+
+
+def dot(a, b, dims=(((1,), (0,)), ((), ()))):
+    return lax.dot_general(a, b, dims, preferred_element_type=jnp.float32)
+
+
+def flat(value):
+    return value.reshape(-1, value.shape[-1])
+
+
+def at(t, size=TILE):
+    return pl.ds(pl.multiple_of(t * size, size), size)
+
+
+def remote(src, dst, send, recv, device):
+    return pltpu.make_async_remote_copy(
+        src_ref=src, dst_ref=dst, send_sem=send, recv_sem=recv, device_id=device, device_id_type=MESH
+    )
+
+
+class Place:
+    def __init__(self, line):
+        dp, fs = lax.axis_index("dp"), lax.axis_index("fsdp")
+        self.line, self.dp, self.fs = line, dp, fs
+        self.x, self.c = dp // 2, dp % 2
+        self.z, self.y = fs // 2, fs % 2
+        self.up, self.down = (dp, fs + 2), (dp, fs - 2)
+        self.yway = (dp, self.z * 2 + 1 - self.y)
+        self.xway = ((1 - self.x) * 2 + self.c, fs)
+        self.core = (self.x * 2 + 1 - self.c, fs)
+        self.has_up, self.has_down = self.z + 1 < line, self.z > 0
+
+    def others(self):
+        return [lax.rem(self.fs + step, 2 * self.line) for step in range(1, 2 * self.line)]
+
+    def greet(self):
+        barrier = pltpu.get_barrier_semaphore()
+        known = [(self.dp, other) for other in self.others()] + [self.xway, self.core]
+        for device in known:
+            pl.semaphore_signal(barrier, inc=1, device_id=device, device_id_type=MESH)
+        pl.semaphore_wait(barrier, len(known))
+
+
+class Panel:
+    def __init__(self, which, part, width):
+        self.which, self.part, self.width = which, part, width
+
+    def cols(self, x):
+        base = 0 if self.which == 3 else self.part * self.width
+        if x is None:
+            return pl.ds(base, self.width)
+        half = self.width // 2
+        return pl.ds(pl.multiple_of(base + x * half, 128), half)
+
+    def of(self, ref, *lead, x=None):
+        if self.which == 3:
+            return ref.at[(*lead, self.part, ALL, self.cols(x))]
+        return ref.at[(*lead, ALL, self.cols(x))]
+
+
+def panels_of(layer_shapes, width, order):
+    made = []
+    for which in order:
+        count = layer_shapes[which]
+        made += [Panel(which, part, width) for part in range(count)]
+    return made
+
+
+class Gather:
+    def __init__(self, at, place, own, panel, full, split, send, recv, near):
+        self.at, self.place, self.own, self.panel, self.full = at, place, own, panel, full
+        self.send, self.recv, self.near = send, recv, near
+        self.split = split
+        self.lane = place.x if split else None
+
+    def view(self, block, y, c, x=None):
+        return self.panel.of(self.full, block, y, c, x=x)
+
+    def sent(self, slot):
+        return self.send.at[self.at, slot]
+
+    def got(self, slot):
+        return self.recv.at[self.at, slot]
+
+    def line_copy(self, way, block):
+        p = self.place
+        ref = self.view(block, p.y, p.c, self.lane)
+        return remote(ref, ref, self.sent(way * p.line + block), self.got(block), (p.up, p.down)[way])
+
+    def near_copy(self):
+        p = self.place
+        mine = self.panel.of(self.own, p.c, x=self.lane)
+        return pltpu.make_async_copy(mine, self.view(p.z, p.y, p.c, self.lane), self.near.at[self.at])
+
+    def far_copy(self, kind):
+        p, line = self.place, self.place.line
+        ref, device = {
+            "y": (lambda: (self.view(ALL, p.y, p.c, p.x), p.yway)),
+            "x": (lambda: (self.view(ALL, 1 - p.y, p.c, p.x), p.xway)),
+            "x_own": (lambda: (self.view(ALL, p.y, p.c, p.x), p.xway)),
+            "core_own": (lambda: (self.view(ALL, p.y, p.c), p.core)),
+            "core": (lambda: (self.view(ALL, 1 - p.y, p.c), p.core)),
+        }[kind]()
+        slot = ("y", "x", "x_own", "core_own", "core").index(kind)
+        return remote(ref, ref, self.sent(2 * line + slot), self.got(line + slot), device)
+
+    def landed(self, kind):
+        p, line = self.place, self.place.line
+        ref = {
+            "y": lambda: self.view(ALL, 1 - p.y, p.c, p.x),
+            "x": lambda: self.view(ALL, 1 - p.y, p.c, 1 - p.x),
+            "x_own": lambda: self.view(ALL, p.y, p.c, 1 - p.x),
+            "core_own": lambda: self.view(ALL, p.y, 1 - p.c),
+            "core": lambda: self.view(ALL, 1 - p.y, 1 - p.c),
+        }[kind]()
+        slot = ("y", "x", "x_own", "core_own", "core").index(kind)
+        return remote(ref, ref, self.sent(2 * line + slot), self.got(line + slot), p.core)
+
+    def kinds(self):
+        return ("y", "x", "x_own", "core_own", "core") if self.split else ("y", "x", "core_own", "core")
+
+    def first(self):
+        p = self.place
+        self.near_copy().start()
+        mine = self.panel.of(self.own, p.c, x=self.lane)
+        there = self.view(p.z, p.y, p.c, self.lane)
+        for way, able, device in ((0, p.has_up, p.up), (1, p.has_down, p.down)):
+            copy = functools.partial(remote, mine, there, self.sent(way * p.line + p.z), self.got(p.z), device)
+            pl.when(able)(lambda copy=copy: copy().start())
+
+    def hop(self, k):
+        p = self.place
+
+        def pass_on(way, block, more):
+            self.line_copy(way, block).wait_recv()
+            pl.when(more)(lambda: self.line_copy(way, block).start())
+
+        pl.when(p.z - k >= 0)(lambda: pass_on(0, p.z - k, p.has_up))
+        pl.when(p.z + k < p.line)(lambda: pass_on(1, p.z + k, p.has_down))
+        if k == p.line - 1:
+            self.near_copy().wait()
+            self.far_copy("y").start()
+            self.far_copy("x_own" if self.split else "core_own").start()
+
+    def cross(self):
+        self.landed("y").wait_recv()
+        self.far_copy("x").start()
+        if self.split:
+            self.landed("x_own").wait_recv()
+            self.far_copy("core_own").start()
+
+    def share(self):
+        self.landed("x").wait_recv()
+        self.far_copy("core").start()
+
+    def stages(self):
+        hops = [functools.partial(self.hop, k) for k in range(1, self.place.line)]
+        return [self.first, *hops, self.cross, self.share]
+
+    def arrive(self):
+        self.landed("core_own").wait_recv()
+        self.landed("core").wait_recv()
+
+    def drain(self):
+        p = self.place
+
+        def body(block, carry):
+            pl.when(p.has_up & (block <= p.z))(lambda: self.line_copy(0, block).wait_send())
+            pl.when(p.has_down & (block >= p.z))(lambda: self.line_copy(1, block).wait_send())
+            return carry
+
+        lax.fori_loop(0, p.line, body, 0)
+        for kind in self.kinds():
+            self.far_copy(kind).wait_send()
+
+
+RINGS = dict(own=10, away=5, other=3, from_x=3, from_y=3, line_in=4, last=3, total=3)
+CREDITS = ("other", "from_x", "from_y", "line_up", "line_down", "last")
+
+
+class Reduce:
+    def __init__(self, at, count, place, panel, terms, out, bufs, credit, send, recv, near):
+        self.at, self.count, self.place, self.panel, self.terms, self.out = at, count, place, panel, terms, out
+        self.credit, self.send, self.recv, self.near = credit, send, recv, near
+        self.b = {name: ref.at[at % RINGS[name]] for name, ref in bufs.items()}
+        self.half = panel.width // 2
+
+    def cols_of(self, x):
+        return pl.ds(pl.multiple_of(x * self.half, 128), self.half)
+
+    def spend(self, name, ring):
+        if self.at >= RINGS[ring]:
+            pl.semaphore_wait(self.credit.at[CREDITS.index(name)], 1)
+
+    def grant(self, name, ring, device):
+        if self.at + RINGS[ring] < self.count:
+            pl.semaphore_signal(
+                self.credit.at[CREDITS.index(name)], inc=1, device_id=device, device_id_type=MESH
+            )
+
+    def sems(self, slot):
+        return self.send.at[self.at, slot], self.recv.at[self.at, slot]
+
+    def core_copy(self):
+        p = self.place
+        return remote(self.panel.of(self.terms, ALL, ALL, 1 - p.c), self.b["other"], *self.sems(0), p.core)
+
+    def near_copy(self, away):
+        p = self.place
+        src = self.panel.of(self.terms, ALL, (1 - p.y) if away else p.y, p.c)
+        return pltpu.make_async_copy(src, self.b["away" if away else "own"], self.near.at[self.at, int(away)])
+
+    def x_copy(self):
+        p = self.place
+        return remote(self.b["away"].at[:, :, self.cols_of(1 - p.x)], self.b["from_x"], *self.sems(1), p.xway)
+
+    def y_copy(self):
+        p = self.place
+        return remote(self.b["away"].at[:, :, self.cols_of(p.x)], self.b["from_y"], *self.sems(2), p.yway)
+
+    def came(self, way, block):
+        return self.b["line_in"].at[block - 1 if way == 0 else self.place.line - 1 + block]
+
+    def line_copy(self, way, block):
+        p = self.place
+        slot = 5 + way * p.line + block
+        return remote(self.b["own"].at[block], self.came(way, block), *self.sems(slot), (p.up, p.down)[way])
+
+    def last_copy(self):
+        p = self.place
+        return remote(self.b["own"].at[p.z], self.b["last"], *self.sems(3), p.xway)
+
+    def out_copy(self):
+        ref = self.panel.of(self.out, self.place.c)
+        return remote(self.b["total"], ref, *self.sems(4), self.place.core)
+
+    def out_landed(self):
+        ref = self.panel.of(self.out, 1 - self.place.c)
+        return remote(self.b["total"], ref, *self.sems(4), self.place.core)
+
+    def out_near(self):
+        return pltpu.make_async_copy(self.b["total"], self.panel.of(self.out, self.place.c), self.near.at[self.at, 2])
+
+    def each(self, body):
+        def step(block, carry):
+            body(block)
+            return carry
+
+        lax.fori_loop(0, self.place.line, step, 0)
+
+    def start(self):
+        self.spend("other", "other")
+        self.core_copy().start()
+        self.near_copy(False).start()
+        self.near_copy(True).start()
+
+    def add_core(self):
+        p, b = self.place, self.b
+        self.near_copy(False).wait()
+        self.near_copy(True).wait()
+        self.core_copy().wait_recv()
+
+        def body(block):
+            b["away"][block] = b["away"][block] + b["other"][block, 1 - p.y]
+
+        self.each(body)
+        self.spend("from_x", "from_x")
+        self.x_copy().start()
+
+        def rest(block):
+            b["own"][block] = b["own"][block] + b["other"][block, p.y]
+
+        self.each(rest)
+        self.grant("other", "other", p.core)
+
+    def add_x(self):
+        p, b = self.place, self.b
+        self.x_copy().wait_recv()
+        cols = self.cols_of(p.x)
+
+        def body(block):
+            b["away"][block, :, cols] = b["away"][block, :, cols] + b["from_x"][block]
+
+        self.each(body)
+        self.spend("from_y", "from_y")
+        self.y_copy().start()
+        self.grant("from_x", "from_x", p.xway)
+
+    def add_y(self):
+        p, b = self.place, self.b
+        self.y_copy().wait_recv()
+        cols = self.cols_of(p.x)
+
+        def body(block):
+            b["own"][block, :, cols] = b["own"][block, :, cols] + b["from_y"][block]
+
+        self.each(body)
+        self.grant("from_y", "from_y", p.yway)
+
+    def add_line(self, way, block):
+        self.line_copy(way, block).wait_recv()
+        self.b["own"][block] = self.b["own"][block] + self.came(way, block)[...]
+
+    def line_step(self, k):
+        p, line = self.place, self.place.line
+        if k == 0:
+            pl.when(p.has_up)(lambda: self.spend("line_up", "line_in"))
+            pl.when(p.has_down)(lambda: self.spend("line_down", "line_in"))
+        far = line - 1 - k
+        for way, block, valid, more in ((0, far, far > p.z, p.has_down), (1, k, k < p.z, p.has_up)):
+
+            def body(way=way, block=block, more=more):
+                pl.when(more)(lambda: self.add_line(way, block))
+                self.line_copy(way, block).start()
+
+            pl.when(valid)(body)
+
+    def own_step(self):
+        p = self.place
+        pl.when(p.has_down)(lambda: self.add_line(0, p.z))
+        pl.when(p.has_up)(lambda: self.add_line(1, p.z))
+        self.spend("last", "last")
+        self.last_copy().start()
+        pl.when(p.has_down)(lambda: self.grant("line_up", "line_in", p.down))
+        pl.when(p.has_up)(lambda: self.grant("line_down", "line_in", p.up))
+
+    def finish(self):
+        p, b = self.place, self.b
+        self.last_copy().wait_recv()
+        b["total"][...] = b["own"][p.z].astype(jnp.float32) + b["last"][...].astype(jnp.float32)
+        self.grant("last", "last", p.xway)
+        self.out_copy().start()
+        self.out_near().start()
+
+    def stages(self):
+        steps = [self.start, self.add_core, self.add_x, self.add_y]
+        steps += [functools.partial(self.line_step, k) for k in range(self.place.line - 1)]
+        return steps + [self.own_step, self.finish]
+
+    def free_away(self):
+        self.core_copy().wait_send()
+        self.x_copy().wait_send()
+        self.y_copy().wait_send()
+
+    def free_own(self):
+        p = self.place
+        for block in range(p.line):
+            pl.when(block > p.z)(lambda block=block: self.line_copy(0, block).wait_send())
+            pl.when(block < p.z)(lambda block=block: self.line_copy(1, block).wait_send())
+        self.last_copy().wait_send()
+
+    def free_total(self):
+        self.out_copy().wait_send()
+        self.out_near().wait()
+
+
+class Pump:
+    def __init__(self, units, before=None):
+        self.units, self.steps, self.slot = units, [unit.stages() for unit in units], 0
+        self.deep, self.before = len(self.steps[0]), before
+        self.ready = len(units)
+
+    def total(self):
+        return len(self.units) + self.deep - 1
+
+    def left(self):
+        return self.total() - self.slot
+
+    def pump(self, count=1):
+        for _ in range(count):
+            if self.slot >= self.total():
+                return
+            if self.slot < len(self.units) and self.slot >= self.ready:
+                return
+            for j in [0, *range(self.deep - 1, 0, -1)]:
+                unit = self.slot - j
+                if 0 <= unit < len(self.units):
+                    if self.before is not None:
+                        self.before(unit, j)
+                    self.steps[unit][j]()
+            self.slot += 1
+
+    def pump_to(self, slot):
+        self.pump(max(0, slot - self.slot))
+
+    def done_with(self, unit):
+        self.pump_to(unit + self.deep)
+
+
+class Layer:
+    def __init__(self, n, kept, weights, par, b_up, terms, g_par, g_bup):
+        self.n, self.s = n, kept
+        self.w_qkv, self.w_out, self.w_up, self.w_down = weights
+        self.par, self.b_up = par, b_up
+        self.g_qkv, self.g_out, self.g_up, self.g_down = terms
+        self.g_par, self.g_bup = g_par, g_bup
+        self.width, self.deep = self.w_out.shape[-1], self.w_up.shape[-1]
+        self.pending = [None, None]
+
+    def chunks(self, body):
+        def step(i, carry):
+            body(at(i, CHUNK))
+            return carry
+
+        lax.fori_loop(0, self.n // CHUNK, step, 0)
+
+    def tiles(self, first, last, body):
+        def step(i, carry):
+            body(i)
+            return carry
+
+        lax.fori_loop(first, last, step, 0)
+
+    def row(self, ref, i):
+        return ref[i : i + 1, :]
+
+    def tall_copy(self, ref, slot, t):
+        stage = self.s["stage"].at[slot].reshape(*ref.shape[:4], self.width)
+        cols = at(t, self.width)
+        return pltpu.make_async_copy(stage, ref.at[:, :, :, :, cols], self.s["stage_sem"].at[slot])
+
+    def wide_copy(self, ref, slot, t):
+        stage = self.s["stage"].at[slot].reshape(*ref.shape[1:])
+        return pltpu.make_async_copy(stage, ref.at[t], self.s["stage_sem"].at[slot])
+
+    def put(self, make, slot, t, first, value):
+        held = self.pending[slot]
+        pl.when(t > first)(lambda: make(slot, t - 1).wait())
+        if held is not None:
+            pl.when(t == first)(lambda: held.wait())
+        self.s["stage"][slot] = value.astype(jnp.bfloat16)
+        make(slot, t).start()
+
+    def put_all(self):
+        for slot in range(2):
+            if self.pending[slot] is not None:
+                self.pending[slot].wait()
+            self.pending[slot] = None
+
+    def prepare(self, seg_col, seg_row):
+        s, width = self.s, self.width
+        s["bias"][...] = jnp.where(seg_col[...] == seg_row[...], 0.0, -1e30)
+        s["rows"][0:1, 0:width] = self.par[4:5, :]
+        s["rows"][0:1, width : 2 * width] = jnp.zeros((1, width), jnp.float32)
+        s["rows"][0:1, 2 * width :] = self.par[5:6, :]
+
+    def norm_parts(self, values):
+        center = values - jnp.mean(values, axis=-1, keepdims=True)
+        scale = lax.rsqrt(jnp.mean(center * center, axis=-1, keepdims=True) + 1e-05)
+        return center * scale, scale
+
+    def norm(self, src, dst, which):
+        def body(rows):
+            unit, _ = self.norm_parts(src[rows, :].astype(jnp.float32))
+            dst[rows, :] = (unit * self.row(self.par, which) + self.row(self.par, 2 + which)).astype(jnp.bfloat16)
+
+        self.chunks(body)
+
+    def norm_a(self):
+        self.norm(self.s["x"], self.s["a"], 0)
+
+    def project(self):
+        s = self.s
+        queries = self.width // TILE
+
+        def body(t):
+            scale = jnp.where(t < queries, HEAD ** (-0.5), 1.0)
+            found = dot(s["a"][...], flat(self.w_qkv[:, :, :, :, at(t)])) + s["rows"][0:1, at(t)]
+            s["qkv"][:, at(t)] = (found * scale).astype(jnp.bfloat16)
+
+        self.tiles(0, 3 * queries, body)
+        s["a_t"][...] = s["a"][...].T
+
+    def pair(self, i, which):
+        start = which * self.width + i * 128
+        return self.s["qkv"].at[:, pl.ds(pl.multiple_of(start, 128), 128)]
+
+    def own_lanes(self, value, head):
+        lanes = lax.broadcasted_iota(jnp.int32, value.shape, 1)
+        return jnp.where((lanes < HEAD) == (head == 0), value, jnp.zeros_like(value))
+
+    def attend(self, first, last):
+        s = self.s
+
+        def body(i):
+            q, k, v = (self.pair(i, which) for which in range(3))
+            keys = [self.own_lanes(k[...], head) for head in range(2)]
+            vals = [self.own_lanes(v[...], head) for head in range(2)]
+            for part in range(self.n // TILE):
+                cols = slice(part * TILE, part * TILE + TILE)
+                mixed = None
+                for head in range(2):
+                    scores = dot(keys[head], q[cols, :], NT) + s["bias"][:, cols]
+                    raised = jnp.exp(scores - jnp.max(scores, axis=0, keepdims=True))
+                    share = 1.0 / jnp.sum(raised, axis=0, keepdims=True)
+                    weights = (raised * share).astype(jnp.bfloat16)
+                    s["wt"][2 * i + head, :, cols] = weights
+                    found = dot(vals[head], weights, TN)
+                    mixed = found if mixed is None else mixed + found
+                s["o"][cols, at(i, 128)] = mixed.T.astype(jnp.bfloat16)
+
+        self.tiles(first, last, body)
+
+    def branch(self):
+        s = self.s
+
+        def body(t):
+            found = dot(s["o"][...], flat(self.w_out[:, :, :, :, at(t)])) + self.par[6:7, at(t)]
+            s["h"][:, at(t)] = s["x"][:, at(t)].astype(jnp.float32) + found
+
+        self.tiles(0, self.width // TILE, body)
+        s["o_t"][...] = s["o"][...].T
+
+    def norm_c(self):
+        self.norm(self.s["h"], self.s["c"], 1)
+
+    def up(self, first, last):
+        s = self.s
+
+        def body(t):
+            before = dot(s["c"][...], flat(self.w_up[:, :, :, :, at(t)])) + self.b_up[0:1, at(t)]
+            chance = 0.5 + 0.5 * lax.erf(before * 0.7071067811865476)
+            s["g"][:, at(t)] = (before * chance).astype(jnp.bfloat16)
+            slope = chance + before * (jnp.exp(before * before * -0.5) * 0.3989422804014327)
+            s["du"][:, at(t)] = slope.astype(jnp.bfloat16)
+
+        self.tiles(first, last, body)
+
+    def turn_c(self):
+        self.s["c_t"][...] = self.s["c"][...].T
+
+    def down(self):
+        s = self.s
+
+        def body(t):
+            found = dot(s["g"][...], flat(self.w_down[:, :, :, :, :, at(t)])) + self.par[7:8, at(t)]
+            s["a"][:, at(t)] = (s["h"][:, at(t)] + found).astype(jnp.bfloat16)
+
+        self.tiles(0, self.width // TILE, body)
+
+    def feed_back(self, first, last):
+        s, width = self.s, self.width
+        wide, tall = functools.partial(self.wide_copy, self.g_down), functools.partial(self.tall_copy, self.g_up)
+
+        def body(t):
+            cols = at(t, width)
+            grad = dot(s["dy"][...], flat(self.w_down[t]), NT)
+            low = (grad * s["du"][:, cols].astype(jnp.float32)).astype(jnp.bfloat16)
+            s["du"][:, cols] = low
+            self.g_bup[0:1, cols] = jnp.sum(low.astype(jnp.float32), axis=0, keepdims=True)
+            self.put(wide, 0, t, first, dot(s["g"][:, cols], s["dy"][...], TN))
+            self.put(tall, 1, t, first, dot(s["c_t"][...], low))
+
+        self.tiles(first, last, body)
+        self.pending = [wide(0, last - 1), tall(1, last - 1)]
+
+    def up_back(self):
+        self.s["sums"][...] = dot(self.s["du"][...], flat(self.w_up[...]), NT)
+
+    def norm_back(self, src, which, grad, rest, body_out):
+        def body(rows):
+            unit, scale = self.norm_parts(src[rows, :].astype(jnp.float32))
+            came = grad[rows, :]
+            gained = came * self.row(self.par, which)
+            self.g_par[which : which + 1, :] += jnp.sum(came * unit, axis=0, keepdims=True)
+            self.g_par[2 + which : 3 + which, :] += jnp.sum(came, axis=0, keepdims=True)
+            inner = gained - jnp.mean(gained, axis=-1, keepdims=True)
+            inner = inner - unit * jnp.mean(gained * unit, axis=-1, keepdims=True)
+            body_out(rows, rest[rows, :].astype(jnp.float32) + inner * scale)
+
+        self.chunks(body)
+
+    def norm_c_back(self):
+        s = self.s
+
+        def keep(rows, grad):
+            s["dh"][rows, :] = grad
+            low = grad.astype(jnp.bfloat16)
+            s["c"][rows, :] = low
+            self.g_par[6:7, :] += jnp.sum(low.astype(jnp.float32), axis=0, keepdims=True)
+            self.g_par[7:8, :] += jnp.sum(s["dy"][rows, :].astype(jnp.float32), axis=0, keepdims=True)
+
+        self.norm_back(s["h"], 1, s["sums"], s["dy"], keep)
+
+    def branch_back(self):
+        s = self.s
+        tall = functools.partial(self.tall_copy, self.g_out)
+        self.put(tall, 0, 0, 0, dot(s["o_t"][...], s["c"][...]))
+        self.pending[0] = tall(0, 0)
+        s["a"][...] = dot(s["c"][...], flat(self.w_out[...]), NT).astype(jnp.bfloat16)
+
+    def attend_back(self, first, last):
+        s, width = self.s, self.width
+
+        def body(i):
+            q, k, v = (self.pair(i, which) for which in range(3))
+            came = s["a"].at[:, at(i, 128)]
+            dq = dk = dv = None
+            for head in range(2):
+                vals = self.own_lanes(v[...], head)
+                for part in range(self.n // TILE):
+                    cols = slice(part * TILE, part * TILE + TILE)
+                    grad = dot(vals, came[cols, :], NT)
+                    weights = s["wt"][2 * i + head, :, cols].astype(jnp.float32)
+                    product = weights * grad
+                    inner = jnp.sum(product, axis=0, keepdims=True)
+                    s["ds"][head, :, cols] = (product - weights * inner).astype(jnp.bfloat16)
+                one_q = dot(self.own_lanes(k[...], head), s["ds"][head], TN)
+                one_k = dot(s["ds"][head], self.own_lanes(q[...], head))
+                one_v = dot(s["wt"][2 * i + head], self.own_lanes(came[...], head))
+                dq, dk, dv = (one_q, one_k, one_v) if head == 0 else (dq + one_q, dk + one_k, dv + one_v)
+            s["g"][:, at(i, 128)] = dq.T.astype(jnp.bfloat16) * HEAD ** (-0.5)
+            s["g"][:, pl.ds(pl.multiple_of(width + i * 128, 128), 128)] = dk.astype(jnp.bfloat16)
+            s["g"][:, pl.ds(pl.multiple_of(2 * width + i * 128, 128), 128)] = dv.astype(jnp.bfloat16)
+
+        self.tiles(first, last, body)
+
+    def project_terms(self, first, last):
+        s, width = self.s, self.width
+        tall = functools.partial(self.tall_copy, self.g_qkv)
+        for t in range(first, last):
+            grad = s["g"][:, t * width : (t + 1) * width]
+            if t != 1:
+                row = 4 + t // 2
+                self.g_par[row : row + 1, :] = jnp.sum(grad.astype(jnp.float32), axis=0, keepdims=True)
+            slot = (t + 1) % 2
+            self.put(tall, slot, t, t, dot(s["a_t"][...], grad))
+            self.pending[slot] = tall(slot, t)
+
+    def project_back(self):
+        s = self.s
+        s["sums"][...] = dot(s["g"][:, 0 : 3 * self.width], flat(self.w_qkv[...]), NT)
+
+    def norm_a_back(self):
+        s = self.s
+
+        def keep(rows, grad):
+            s["dh"][rows, :] = grad
+
+        self.norm_back(s["x"], 0, s["sums"], s["dh"], keep)
+
+
+def layer_scratch(n, width, deep):
+    low, full = jnp.bfloat16, jnp.float32
+    return dict(
+        a=pltpu.VMEM((n, width), low),
+        a_t=pltpu.VMEM((width, n), low),
+        qkv=pltpu.VMEM((n, 3 * width), low),
+        bias=pltpu.VMEM((n, n), full),
+        wt=pltpu.VMEM((width // HEAD, n, n), low),
+        ds=pltpu.VMEM((2, n, n), low),
+        o=pltpu.VMEM((n, width), low),
+        o_t=pltpu.VMEM((width, n), low),
+        h=pltpu.VMEM((n, width), full),
+        c=pltpu.VMEM((n, width), low),
+        c_t=pltpu.VMEM((width, n), low),
+        g=pltpu.VMEM((n, deep), low),
+        du=pltpu.VMEM((n, deep), low),
+        sums=pltpu.VMEM((n, width), full),
+        dh=pltpu.VMEM((n, width), full),
+        rows=pltpu.VMEM((8, 3 * width), full),
+        stage=pltpu.VMEM((2, width, width), low),
+        stage_sem=pltpu.SemaphoreType.DMA((2,)),
+    )
+
+
+def cut(kept, n):
+    cuts = dict(kept)
+    for name in ("a", "qkv", "o", "h", "c", "g", "du", "sums", "dh"):
+        cuts[name] = kept[name].at[0:n]
+    for name in ("a_t", "o_t", "c_t"):
+        cuts[name] = kept[name].at[:, 0:n]
+    cuts["bias"] = kept["bias"].at[0:n, 0:n]
+    for name in ("wt", "ds"):
+        cuts[name] = kept[name].at[:, 0:n, 0:n]
+    return cuts
+
+
+ORDER = (0, 1, 2, 3)
+BACK = (3, 2, 1, 0)
+
+
+class SmallSum:
+    def __init__(self, place, parts, land, line_land, out, send, recv):
+        self.place, self.parts, self.land, self.line_land, self.out = place, parts, land, line_land, out
+        self.send, self.recv = send, recv
+
+    def near(self, step):
+        p = self.place
+        device = (p.core, p.xway, p.yway)[step]
+        return remote(self.parts.at[step], self.land.at[step], self.send.at[step], self.recv.at[step], device)
+
+    def far(self, step):
+        p = self.place
+        other = lax.rem(p.z + step, p.line)
+        device = (p.dp, other * 2 + p.y)
+        src = self.parts.at[3]
+        return remote(src, self.line_land.at[p.z], self.send.at[3 + other], self.recv.at[3 + p.z], device)
+
+    def from_far(self, step):
+        p = self.place
+        other = lax.rem(p.z + step, p.line)
+        device = (p.dp, other * 2 + p.y)
+        src = self.parts.at[3]
+        return remote(src, self.line_land.at[other], self.send.at[3 + other], self.recv.at[3 + other], device)
+
+    def stage(self, step):
+        p = self.place
+        if step:
+            if step <= 3:
+                self.near(step - 1).wait_recv()
+                self.parts[step] = self.parts[step - 1] + self.land[step - 1]
+        if step < 3:
+            self.near(step).start()
+        if step == 3:
+            for other in range(1, p.line):
+                self.far(other).start()
+            self.line_land[p.z] = self.parts[3]
+        if step == 4:
+            for other in range(1, p.line):
+                self.from_far(other).wait_recv()
+            total = self.line_land[0]
+            for block in range(1, p.line):
+                total = total + self.line_land[block]
+            self.out[...] = total
+            for near in range(3):
+                self.near(near).wait_send()
+            for other in range(1, p.line):
+                self.far(other).wait_send()
+
+
+def whole_kernel(line, sizes, names, ring_names, splits, *refs):
+    take = list(refs)
+
+    def some(count):
+        found = take[:count]
+        del take[:count]
+        return found
+
+    owned, (small,) = some(4), some(1)
+    x_t, dy_t, col_t, row_t, x_i, dy_i, col_i, row_i = some(8)
+    y_i, y_t, gx_i, gx_t = some(4)
+    shares, (small_out,) = some(4), some(1)
+    far_weights, terms_t, terms_i = some(4), some(4), some(4)
+    weights = some(4)
+    kept = dict(zip(names, some(len(names))))
+    bufs = dict(zip(ring_names, some(len(ring_names))))
+    pad_x, pad_dy, small_all, par, b_up, g_parts, g_land, g_line = some(8)
+    ag_send, ag_recv, ag_near, rs_send, rs_recv, rs_near, credit = some(7)
+    s_send, s_recv, g_send, g_recv, load_sem, io_sem = some(6)
+    n_t, n_i, counts = sizes
+    width = weights[1].shape[-1]
+    place = Place(line)
+    place.greet()
+
+    first = panels_of(counts, width, ORDER)
+    units = [
+        Gather(u, place, owned[p.which].at[1], p, weights[p.which], u in splits, ag_send, ag_recv, ag_near)
+        for u, p in enumerate(first)
+    ]
+    base = len(first)
+    units += [
+        Gather(base + u, place, owned[p.which].at[0], p, far_weights[p.which], base + u in splits, ag_send, ag_recv, ag_near)
+        for u, p in enumerate(first)
+    ]
+    ag = Pump(units)
+    back = panels_of(counts, width, BACK)
+    sums = []
+    for u, p in enumerate(back + back):
+        layer = 1 if u < len(back) else 0
+        terms = (terms_i, terms_t)[layer]
+        sums.append(
+            Reduce(u, 2 * len(back), place, p, terms[p.which], shares[p.which].at[layer], bufs, credit, rs_send, rs_recv, rs_near)
+        )
+
+    def before(unit, stage):
+        last = len(sums[0].stages()) - 1
+        if stage == 0:
+            if unit >= RINGS["away"]:
+                sums[unit - RINGS["away"]].free_away()
+            if unit >= RINGS["own"]:
+                sums[unit - RINGS["own"]].free_own()
+        if stage == last and unit >= RINGS["total"]:
+            sums[unit - RINGS["total"]].free_total()
+
+    rs = Pump(sums, before)
+    rs.ready = 0
+
+    def both(count=1, more=1):
+        for _ in range(max(count, more)):
+            if count > 0:
+                ag.pump(1)
+            if more > 0:
+                rs.pump(1)
+            count, more = count - 1, more - 1
+
+    smalls = []
+    for step, other in enumerate(place.others()):
+        smalls.append(
+            remote(small, small_all.at[place.fs], s_send.at[step], s_recv.at[place.fs], (place.dp, other))
+        )
+        smalls[-1].start()
+    ag.pump(1)
+    small_all[place.fs] = small[...]
+    g_parts[0] = jnp.zeros(g_parts.shape[1:], jnp.float32)
+    ag.pump(1)
+    for step, other in enumerate(place.others()):
+        remote(small, small_all.at[other], s_send.at[step], s_recv.at[other], (place.dp, other)).wait_recv()
+    piece, deep = width // (2 * line), b_up.shape[-1] // (2 * line)
+    for layer in range(2):
+        for block in range(2 * line):
+            par[layer, :, block * piece : (block + 1) * piece] = small_all[block, layer, 0:8, 0:piece]
+            for j in range(deep // 128):
+                start = block * deep + j * 128
+                b_up[layer, 0:1, start : start + 128] = small_all[block, layer, 8 + j : 9 + j, :]
+    for copy in smalls:
+        copy.wait_send()
+
+    def layer_of(layer, n, view, terms):
+        return Layer(n, view, weights, par.at[layer], b_up.at[layer], terms, g_parts.at[0, layer, 0:8], g_bup.at[layer])
+
+    g_bup = b_up.at[2:4]
+    starts = [sum(counts[:which]) for which in range(5)]
+
+    text = layer_of(1, n_t, {**kept, "x": x_t.at[0], "dy": dy_t.at[0]}, terms_t)
+    text.prepare(col_t, row_t)
+    text.norm_a()
+
+    def need(unit):
+        ag.done_with(unit)
+        units[unit].arrive()
+
+    for unit in range(starts[0], starts[1]):
+        need(unit)
+    text.project()
+    heads = width // 128
+    for i in range(0, heads, 2):
+        text.attend(i, i + 2)
+        ag.pump(1)
+    need(starts[1])
+    text.branch()
+    ag.pump(1)
+    text.norm_c()
+    tiles = width // TILE
+    for part in range(counts[2]):
+        need(starts[2] + part)
+        text.up(part * tiles, (part + 1) * tiles)
+    text.turn_c()
+    for part in range(counts[3]):
+        need(starts[3] + part)
+    text.down()
+    y_copy = pltpu.make_async_copy(kept["a"], y_t.at[0], io_sem.at[0])
+    y_copy.start()
+    ag.pump(1)
+    panels = counts[3]
+    text.feed_back(0, panels // 2)
+    ag.pump(2)
+    text.feed_back(panels // 2, panels)
+    text.put_all()
+    rs.ready = counts[3] + counts[2]
+    both()
+    text.up_back()
+    both()
+    text.norm_c_back()
+    both()
+    y_copy.wait()
+    text.branch_back()
+    text.put_all()
+    rs.ready += 1
+    both()
+    for i in range(0, heads, 2):
+        text.attend_back(i, i + 2)
+        both()
+    text.project_terms(0, 3)
+    text.put_all()
+    rs.ready += 3
+    both()
+    text.project_back()
+    both()
+    text.norm_a_back()
+    grad_copy = pltpu.make_async_copy(kept["dh"], gx_t.at[0], io_sem.at[1])
+    grad_copy.start()
+
+    for src, dst in ((x_i, pad_x), (dy_i, pad_dy)):
+        have = src.shape[1]
+        if have < n_i:
+            cut_at = have // 16 * 16
+            dst[cut_at:, :] = jnp.zeros((n_i - cut_at, width), jnp.bfloat16)
+        dst[0:have, :] = src[0]
+    view = {**cut(kept, n_i), "x": pad_x, "dy": pad_dy}
+    image = layer_of(0, n_i, view, terms_i)
+    image.prepare(col_i, row_i)
+    image.norm_a()
+    loads = [pltpu.make_async_copy(far_weights[i], weights[i], load_sem.at[i]) for i in range(4)]
+    for which in range(4):
+        for unit in range(starts[which], starts[which + 1]):
+            need(base + unit)
+            units[unit].drain()
+        loads[which].start()
+    loads[0].wait()
+    image.project()
+    rs.pump(1)
+    image.attend(0, heads)
+    rs.pump(1)
+    loads[1].wait()
+    image.branch()
+    image.norm_c()
+    rs.pump(1)
+    loads[2].wait()
+    image.up(0, counts[2] * tiles)
+    rs.pump(1)
+    image.turn_c()
+    loads[3].wait()
+    image.down()
+    y_i[0] = view["a"][0 : y_i.shape[1], :]
+    rs.pump(1)
+    image.feed_back(0, panels)
+    image.put_all()
+    rs.ready += counts[3] + counts[2]
+    rs.pump(1)
+    image.up_back()
+    rs.pump(1)
+    grad_copy.wait()
+    image.norm_c_back()
+    rs.pump(1)
+    image.branch_back()
+    image.put_all()
+    rs.ready += 1
+    rs.pump(1)
+    image.attend_back(0, heads)
+    rs.pump(1)
+    image.project_terms(0, 3)
+    image.put_all()
+    rs.ready += 3
+    rs.pump(1)
+    image.project_back()
+    rs.pump(1)
+    image.norm_a_back()
+    gx_i[0] = view["dh"][0 : gx_i.shape[1], :]
+    for layer in range(2):
+        for j in range(b_up.shape[-1] // width):
+            g_parts[0, layer, 8 + j : 9 + j, :] = g_bup[layer, 0:1, j * width : (j + 1) * width]
+    small_sum = SmallSum(place, g_parts, g_land, g_line, small_out, g_send, g_recv)
+    for step in range(5):
+        small_sum.stage(step)
+        rs.pump(1)
+    rs.pump(rs.left())
+    total = len(sums)
+    for unit in sums[total - RINGS["away"] :]:
+        unit.free_away()
+    for unit in sums[total - RINGS["own"] :]:
+        unit.free_own()
+    for unit in sums[total - RINGS["total"] :]:
+        unit.free_total()
+    for unit in sums:
+        unit.out_landed().wait_recv()
+    for unit in units[base:]:
+        unit.drain()
+
+
+def padded(rows):
+    return -(-rows // TILE) * TILE
+
+
+def whole(line, x_i, dy_i, x_t, dy_t, seg_i, seg_t, owned, small):
+    width, deep = owned[1].shape[2], owned[2].shape[2]
+    rows = owned[1].shape[1] // 2
+    counts = (3, 1, deep // width, deep // width)
+    own = [w.reshape(2, 2, rows, w.shape[2]) for w in owned[:3]] + [owned[3].reshape(2, 2, counts[3], rows, width)]
+    n_t, n_i = padded(x_t.shape[1]), padded(x_i.shape[1])
+    low, full = jnp.bfloat16, jnp.float32
+    kept = layer_scratch(n_t, width, deep)
+    pads = lambda seg, n: jnp.pad(seg, ((0, 0), (0, n - seg.shape[1])), constant_values=-1)
+    seg_t, seg_i = pads(seg_t, n_t), pads(seg_i, n_i)
+    fulls = [(line, 2, *w.shape[1:]) for w in own]
+    rings = dict(
+        own=pltpu.VMEM((RINGS["own"], line, rows, width), low),
+        away=pltpu.VMEM((RINGS["away"], line, rows, width), low),
+        other=pltpu.VMEM((RINGS["other"], line, 2, rows, width), low),
+        from_x=pltpu.VMEM((RINGS["from_x"], line, rows, width // 2), low),
+        from_y=pltpu.VMEM((RINGS["from_y"], line, rows, width // 2), low),
+        line_in=pltpu.VMEM((RINGS["line_in"], 2 * line - 2, rows, width), low),
+        last=pltpu.VMEM((RINGS["last"], rows, width), low),
+        total=pltpu.VMEM((RINGS["total"], rows, width), full),
+    )
+    panels = 2 * sum(counts)
+    splits = ()
+    small_rows = 8 + deep // width
+    small_rows += -small_rows % 8
+    anywhere, inside = pl.BlockSpec(memory_space=pl.ANY), pl.BlockSpec(memory_space=pltpu.VMEM)
+    dma = pltpu.SemaphoreType.DMA
+    outs = [
+        jax.ShapeDtypeStruct(x_i.shape, low),
+        jax.ShapeDtypeStruct(x_t.shape, low),
+        jax.ShapeDtypeStruct(x_i.shape, full),
+        jax.ShapeDtypeStruct(x_t.shape, full),
+        *[jax.ShapeDtypeStruct(w.shape, full) for w in own],
+        jax.ShapeDtypeStruct((2, small_rows, width), full),
+        *[jax.ShapeDtypeStruct(shape, low) for shape in fulls * 3],
+    ]
+    scratch = [
+        *[pltpu.VMEM(shape, low) for shape in fulls],
+        *kept.values(),
+        *rings.values(),
+        pltpu.VMEM((n_i, width), low),
+        pltpu.VMEM((n_i, width), low),
+        pltpu.VMEM((2 * line, *small.shape), full),
+        pltpu.VMEM((2, 8, width), full),
+        pltpu.VMEM((4, 1, deep), full),
+        pltpu.VMEM((4, 2, small_rows, width), full),
+        pltpu.VMEM((3, 2, small_rows, width), full),
+        pltpu.VMEM((line, 2, small_rows, width), full),
+        dma((panels, 2 * line + 5)),
+        dma((panels, line + 5)),
+        dma((panels,)),
+        dma((panels, 5 + 2 * line)),
+        dma((panels, 5 + 2 * line)),
+        dma((panels, 3)),
+        pltpu.SemaphoreType.REGULAR((len(CREDITS),)),
+        dma((2 * line,)),
+        dma((2 * line,)),
+        dma((3 + line,)),
+        dma((3 + line,)),
+        dma((4,)),
+        dma((2,)),
+    ]
+    found = pl.pallas_call(
+        functools.partial(whole_kernel, line, (n_t, n_i, counts), list(kept), list(rings), splits),
+        out_shape=outs,
+        in_specs=[anywhere] * 4 + [inside] * 9,
+        out_specs=[inside, anywhere, inside, anywhere] + [anywhere] * 4 + [inside] + [anywhere] * 12,
+        scratch_shapes=scratch,
+        compiler_params=pltpu.CompilerParams(collective_id=0, has_side_effects=True, vmem_limit_bytes=63 * 2**20),
+    )(*own, small, x_t, dy_t, seg_t.reshape(n_t, 1), seg_t, x_i, dy_i, seg_i.reshape(n_i, 1), seg_i)
+    shares = [share.reshape(w.shape) for share, w in zip(found[4:8], owned)]
+    return found[:4], shares, found[8]
 
 
 def normed(values, gain, shift):
@@ -195,6 +1242,7 @@
         ]
     )
     return (
+        result.astype(jnp.bfloat16),
         grad_inputs,
         (grad_qkvw, grad_outw, grad_upw, grad_downw, grad_gains, grad_biases, grad_upb),
     )
@@ -282,7 +1330,7 @@
     )
 
 
-def local(
+def plain(
     images,
     image_cot,
     captions,
@@ -304,13 +1352,40 @@
     second_weights = fetch_weights(1, *owned)
     caption_out = forward_layer(captions, second_weights, caption_seg)[-1].astype(jnp.bfloat16)
     second_back = fetch_again(1, *owned)
-    caption_grad, caption_terms = backward_layer(captions, caption_cot, second_back, caption_seg)
+    _, caption_grad, caption_terms = backward_layer(captions, caption_cot, second_back, caption_seg)
     caption_shares = reduce_grads(caption_terms)
     first_back = fetch_again(0, *owned)
-    image_grad, image_terms = backward_layer(images, image_cot, first_back, image_seg)
+    _, image_grad, image_terms = backward_layer(images, image_cot, first_back, image_seg)
     image_shares = reduce_grads(image_terms)
     stacked = tuple((jnp.stack([image_shares[index], caption_shares[index]]) for index in range(7)))
     return (image_out, caption_out, image_grad, caption_grad) + stacked
+
+
+def kernels_fit(mesh, w_qkv):
+    return mesh.shape["dp"] == 4 and mesh.shape["fsdp"] % 2 == 0 and w_qkv.shape[1] % 32 == 0
+
+
+def local(mesh, images, image_cot, captions, caption_cot, lengths, w_qkv, w_out, w_up, w_down, gains, biases, b_up):
+    if not kernels_fit(mesh, w_qkv):
+        return plain(
+            images, image_cot, captions, caption_cot, lengths, w_qkv, w_out, w_up, w_down, gains, biases, b_up
+        )
+    line, width = mesh.shape["fsdp"] // 2, gains.shape[2]
+    deep = b_up.shape[1]
+    par = jnp.concatenate([gains, biases], axis=1)
+    par = jnp.pad(par, ((0, 0), (0, 0), (0, -width % 128)))
+    small = jnp.concatenate([par, b_up.reshape(2, deep // 128, 128)], axis=1).astype(jnp.float32)
+    small = jnp.pad(small, ((0, 0), (0, -small.shape[1] % 8), (0, 0)))
+    image_seg = jnp.zeros((images.shape[0], images.shape[1]), jnp.int32)
+    caption_seg = segment_ids(lengths, captions.shape[1])
+    outs, shares, sums = whole(
+        line, images, image_cot, captions, caption_cot, image_seg, caption_seg, (w_qkv, w_out, w_up, w_down), small
+    )
+    place = lax.axis_index("fsdp")
+    mine = lax.dynamic_slice_in_dim(sums[:, :8], place * width, width, 2)
+    up = sums[:, 8 : 8 + deep * 2 * line // w_out.shape[2]].reshape(2, -1)
+    up = lax.dynamic_slice_in_dim(up, place * deep, deep, 1)
+    return (*outs, *shares, mine[:, :2], mine[:, 2:], up)
 
 
 def solution(mesh):
@@ -329,7 +1404,7 @@
         P(None, "fsdp"),
     )
     return jax.shard_map(
-        local,
+        functools.partial(local, mesh),
         mesh=mesh,
         in_specs=placed,
         out_specs=(

time: 2100 us -> 459 us (0.22)
  waiting for transfers between devices: 1480 us -> 0 us
  Pallas kernels: 0 us -> 427 us
  blocking collectives: 274 us -> 0 us
  matrix products: 170 us -> 0 us
  other arithmetic: 97.4 us -> 2.22 us
  local copies, waits for them, and re-layouts: 48.3 us -> 20.9 us
    reduce_scatter x16 -> x0, waiting for transfers between devices: 987 us -> none  [the longest x2 313 us: reduce_grads(): lax.psum_scatter(gradients[2], 'fsdp', scatter_dimension=0, tiled=True)]
    pallas_call x0 -> x1, Pallas kernels: none -> 427 us  [whole(): pl.pallas_call(functools.partial(whole_kernel, line, (n_t, n_i, counts),...]
    all_gather x8 -> x0, waiting for transfers between devices: 255 us -> none  [the longest x2 130 us: fetch_weights(): lax.all_gather(w_down[layer_index], 'fsdp', axis=0, tiled=True)]
    unnamed x32 -> x0, waiting for transfers between devices: 242 us -> none
    all_gather x18 -> x0, blocking collectives: 225 us -> none  [the longest x2 53.2 us: fetch_weights(): lax.all_gather(biases[layer_index], 'fsdp', axis=1, tiled=True)]
    dot_general x36 -> x0, matrix products: 170 us -> none  [the longest x2 30.9 us: forward_layer(): jnp.einsum('bld,df->blf', normed_c, up_weight, preferred_element_type=jnp...]
    convert_element_type x18 -> x0, other arithmetic: 64.4 us -> none  [the longest x2 28 us: forward_layer(): hidden + jnp.einsum('blf,fd->bld', activated, down_weight, preferred_elem...]
    unnamed x3 -> x0, blocking collectives: 49 us -> none
  transfers between devices with their start and end apart: 28 -> 0, of which waited for: 22 -> 0; matrix products, arithmetic and copies ran while one was open for 14% -> 0% of each run, Pallas kernels for 0% -> 0%
where the time goes in v4:
time: 459 us; the launch traced here: 451 us
  Pallas kernels  427 us (93%)
  local copies, waits for them, and re-layouts  20.9 us (5%)
    pallas_call x1, Pallas kernels, whole(): pl.pallas_call(functools.partial(whole_kernel, line, (n_t, n_i, counts),...  427 us
    unnamed x26, local copies, waits for them, and re-layouts  16.3 us

profile of v4, /device:TPU:9, one launch (start us, length us, event | category | flops | bytes accessed | tf_op | source)
XLA Modules:
  0.0 450.9 jit_solution(8843811781006760022)
XLA Ops:
  0.6 0.8 reduce_window_sum.11
  1.5 0.1 convert_reduce_fusion
  1.6 0.0 copy-start.5
  1.6 0.9 copy.32.refs_7_
  2.4 0.8 copy.33.refs_11_
  3.2 0.7 copy.31
  3.9 0.7 fusion.6
  4.6 0.7 reshape.112
  5.3 0.6 fusion.3.refs_4_
  5.9 0.0 copy-done.5
  5.9 0.0 copy-done.6
  5.9 426.7 %shard_map.203 = (bf16[1,197,768]{2,1,0:T(8,128)(2,1)}, bf16[1,512,768]{2,1,0:T(8,128)(2,1)}, f32[1,197,768]{2,1,0:T(8,128)}, f32[1,512,768]{2,1,0:T(8,128)}, f3...) custom-call(bf16[2,2,48,2304]{3,2,1,0:T(8,128)(2,1)} %bitcast.21, ...), custom_call_target="tpu_custom_call" | custom-call | tf_op jit(solution)/shard_map/pallas_call | solution.py:1044
  432.7 0.0 copy-start.3
  432.7 0.9 slice.12
  433.6 0.1 constant_dynamic-slice_fusion.2
  433.7 0.6 copy.35
  434.3 0.7 constant_dynamic-slice_fusion
  434.9 0.8 slice_bitcast_fusion
  435.7 0.6 constant_dynamic-slice_fusion.1
  436.3 2.5 copy.34
  438.8 1.7 copy.44
  440.5 2.2 copy.45
  442.7 0.0 copy-done.3
  442.7 1.1 copy.46
  443.9 0.0 copy-done.2
  443.9 1.2 copy.47
  445.1 0.2 copy-done.4
  445.3 0.8 copy.48
  446.1 0.4 copy-done.1
  446.6 1.4 copy.49
  448.0 1.1 copy-done
  449.1 1.4 copy.50
  (8 shorter events, 0.0 us)
Async XLA Ops:
  1.6 4.4 copy-start.5
  2.4 3.5 copy-start.6
  432.7 10.1 %copy-start.3 = (f32[1,512,768]{2,1,0:T(8,128)S(1)}, f32[1,512,768]{2,1,0:T(8,128)}, u32[]{:S(2)}) copy-start(f32[1,512,768]{2,1,0:T(8,128)} %get-tuple-element.76) | copy-start | bytes 4718596
  440.5 3.3 copy-start.2
  443.9 1.4 copy-start.4
  443.9 2.7 copy-start.1
  446.6 2.5 copy-start
